TPU v7x, 256 devices: a whole 4x4x8 slice. The times are simulated.
256 devices in a mesh: dom: 64 (over x, y, z_hi), sub: 4 (over z_lo, core).
Axes of the slice: x: 4, y: 4, z: 8 (z_hi: 4, z_lo: 2; z = z_hi * 2 + z_lo), core: 2. Of those that a mesh axis runs over, the one named last changes fastest.
Arguments:
- features: bfloat16 [64, 4, 2048, 128], P('dom', 'sub'), may hold values from -6 to 6
- offsets: int32 [3, 64, 4, 2048], P(None, 'dom', 'sub'), may hold values from 0 to 255, as said below
- frac: float32 [3, 64, 4, 2048], P(None, 'dom', 'sub'), may hold values from 0 to 0.999
- neighbors: int32 [64, 4, 2048, 16], P('dom', 'sub'), may hold values from 0 to 6143, as said below
- counts: int32 [64, 4, 2048], P('dom', 'sub'), may hold values from 1 to 16, as said below
- w_src: bfloat16 [128, 128], replicated, may hold values from -0.5 to 0.5
- w_dst: bfloat16 [128, 128], replicated, may hold values from -0.5 to 0.5
- w_rad: float32 [8, 128], replicated, may hold values from -3 to 3
- w_mid: bfloat16 [128, 128], replicated, may hold values from -0.5 to 0.5
- w_out: bfloat16 [384, 128], replicated, may hold values from -0.5 to 0.5
- w_charge: float32 [128], replicated, may hold values from -0.5 to 0.5
Outputs:
- new_features: bfloat16 [64, 4, 2048, 128], P('dom', 'sub')
- potential: float32 [64, 4, 2048], P('dom', 'sub')
Inputs may be any that keep to these rules, and one draw needn't show every extreme that they name: `offsets`: component 0 of an atom of block (b, c) lies in [b * 4, (b + 1) * 4), component 1 in [c * 64, (c + 1) * 64). `neighbors`: an entry below 2048 names another atom of the same block, never the atom itself; a larger entry 2048 + r * 512 + s names atom s of the r-th of the eight surrounding blocks, taken in row-major order of their displacement along dom and sub with wrap-around; slot 0 of the first atom of every block holds the largest value. Slots at positions counts and later are padding; the first atom of every block has 16 live slots.
All inputs are finite; a program needn't handle non-finite values.
Results may differ from a plain program's by a relative error of at most 0.0052.
Values may be sent and summed in bfloat16 or wider, within the bound.
A program may use at most 128 MiB of HBM per device.

v0:
```python
import math

import jax
import jax.numpy as jnp
from jax import lax
from jax.sharding import PartitionSpec as P

GRID = 256


beta_ewald = 1.0
pot_scale = 16.0
cut_radius = 64.0
highest = lax.Precision.HIGHEST


def extended(x, sides, width):
    for axis, dim in sides:
        size, length = (lax.axis_size(axis), x.shape[dim])
        up = [(i, (i + 1) % size) for i in range(size)]
        down = [(j, i) for i, j in up]
        last = lax.slice_in_dim(x, length - width, length, axis=dim)
        first = lax.slice_in_dim(x, 0, width, axis=dim)
        before = lax.ppermute(last, axis, up)
        after = lax.ppermute(first, axis, down)
        x = jnp.concatenate([before, x, after], axis=dim)
    return x


def spline_weight(argument):
    cube_value = argument * argument * argument
    piece_one = cube_value / 6.0
    second = (-3.0 * cube_value + 12.0 * argument * argument - 12.0 * argument + 4.0) / 6.0
    piece_three = (3.0 * cube_value - 24.0 * argument * argument + 60.0 * argument - 44.0) / 6.0
    remain = 4.0 - argument
    fourth = remain * remain * remain / 6.0
    result = jnp.where(
        argument < 1.0,
        piece_one,
        jnp.where(argument < 2.0, second, jnp.where(argument < 3.0, piece_three, fourth)),
    )
    return jnp.where((argument >= 0.0) & (argument < 4.0), result, jnp.zeros_like(result))


def wrap_cells(delta_cells, length):
    return (delta_cells + length // 2) % length - length // 2


def harmonics(direction):
    axis_x, axis_y, axis_z = (direction[0], direction[1], direction[2])
    root_three = math.sqrt(3.0)
    root_five = math.sqrt(5.0)
    root_fifteen = math.sqrt(15.0)
    return jnp.stack(
        [
            jnp.ones_like(axis_x),
            root_three * axis_x,
            root_three * axis_y,
            root_three * axis_z,
            root_fifteen * axis_x * axis_y,
            root_fifteen * axis_y * axis_z,
            0.5 * root_five * (3.0 * axis_z * axis_z - 1.0),
            root_fifteen * axis_x * axis_z,
            0.5 * root_fifteen * (axis_x * axis_x - axis_y * axis_y),
        ]
    )


def edge_update(own_rows, src_term, dst_term, displace, live_slot, w_rad, w_mid, w_out):
    distance = jnp.sqrt(jnp.sum(displace * displace, axis=0) + 1.0)
    direction = displace / distance
    envelope = jnp.where(live_slot, 1.0 / (1.0 + (distance / cut_radius) ** 2), 0.0)
    lengths = 2.0 ** jnp.arange(w_rad.shape[0], dtype=jnp.float32)
    radial = jnp.exp(-distance[..., None] / lengths)
    radial_term = jnp.einsum("akn,nc->akc", radial, w_rad, precision=highest)
    latent = jax.nn.silu(src_term[:, None, :] + dst_term + radial_term).astype(jnp.bfloat16)
    hidden = jax.nn.silu(
        jnp.einsum("akc,cd->akd", latent, w_mid, preferred_element_type=jnp.float32)
    )
    message = hidden * envelope[..., None]
    angular = harmonics(direction)
    moments = jnp.einsum("akc,mak->amc", message, angular, precision=highest)
    invariant = jnp.concatenate(
        [
            moments[:, 0] ** 2,
            jnp.sum(moments[:, 1:4] ** 2, axis=1),
            jnp.sum(moments[:, 4:9] ** 2, axis=1),
        ],
        axis=-1,
    ).astype(jnp.bfloat16)
    update = jnp.dot(invariant, w_out, preferred_element_type=jnp.float32)
    return (own_rows.astype(jnp.float32) + update).astype(jnp.bfloat16)


def influence_axis(indices):
    signed = ((indices + GRID // 2) % GRID - GRID // 2).astype(jnp.float32) / GRID
    factor = (2.0 + jnp.cos(2.0 * math.pi / GRID * indices.astype(jnp.float32))) / 3.0
    return (signed * signed, factor * factor)


def influence_block(index_x, index_y, index_z):
    square_x, factor_x = influence_axis(index_x)
    square_y, factor_y = influence_axis(index_y)
    square_z, factor_z = influence_axis(index_z)
    squared = square_x[:, None, None] + square_y[None, :, None] + square_z[None, None, :]
    damping = factor_x[:, None, None] * factor_y[None, :, None] * factor_z[None, None, :]
    positive = squared > 0.0
    safe_square = jnp.where(positive, squared, 1.0)
    weighted = (
        pot_scale * jnp.exp(-(math.pi**2 / beta_ewald**2) * squared) / (safe_square * damping)
    )
    return jnp.where(positive, weighted, 0.0)


def dft_tables(length):
    indices = jnp.arange(length, dtype=jnp.int32)
    phase = indices[:, None] * indices[None, :] % length
    angle = 2.0 * math.pi / length * phase.astype(jnp.float32)
    return (jnp.cos(angle), jnp.sin(angle))


def complex_step(spectrum, cos_table, sin_table, pattern, direction_sign):
    real_part = jnp.einsum(
        pattern, cos_table, spectrum[0], precision=highest
    ) + direction_sign * jnp.einsum(pattern, sin_table, spectrum[1], precision=highest)
    imag_part = jnp.einsum(
        pattern, cos_table, spectrum[1], precision=highest
    ) - direction_sign * jnp.einsum(pattern, sin_table, spectrum[0], precision=highest)
    return jnp.stack([real_part, imag_part])


def swap_sub(spectrum):
    return lax.all_to_all(spectrum, "sub", split_axis=1, concat_axis=3, tiled=True)


def swap_dom(spectrum):
    return lax.all_to_all(spectrum, "dom", split_axis=1, concat_axis=2, tiled=True)


def axis_weights(cell_ids, offset_row, frac_row):
    delta = wrap_cells(offset_row[None, :] - cell_ids[:, None], GRID).astype(jnp.float32)
    return spline_weight(frac_row[None, :] + delta + 2.0)


def local(features, offsets, frac, neighbors, counts, w_src, w_dst, w_rad, w_mid, w_out, w_charge):
    atom_count = features.shape[2]
    channels = features.shape[3]
    rim_rows = atom_count // 4
    dom_count = lax.axis_size("dom")
    sub_count = lax.axis_size("sub")
    own_rows = features[0, 0]
    raw_charge = jnp.dot(own_rows.astype(jnp.float32), w_charge, precision=highest).reshape(
        atom_count // 2, 2
    )
    half_gap = 0.5 * (raw_charge[:, 0] - raw_charge[:, 1])
    charges = jnp.stack([half_gap, -half_gap], axis=1).reshape(atom_count)
    geometry = jnp.concatenate(
        [offsets.astype(jnp.float32), frac, charges.reshape(1, 1, 1, atom_count)], axis=0
    )
    feat_halo = extended(features, (("dom", 0), ("sub", 1)), 1)
    geo_halo = extended(geometry, (("dom", 1), ("sub", 2)), 1)
    halo_places = [(0, 0), (0, 1), (0, 2), (1, 0), (1, 2), (2, 0), (2, 1), (2, 2)]
    own_geom = geometry[0:6, 0, 0]
    feat_table = jnp.concatenate(
        [own_rows] + [feat_halo[place_x, place_y, :rim_rows] for place_x, place_y in halo_places],
        axis=0,
    )
    geo_table = jnp.concatenate(
        [own_geom]
        + [geo_halo[0:6, place_x, place_y, :rim_rows] for place_x, place_y in halo_places],
        axis=1,
    )
    src_rows = jnp.dot(own_rows, w_src, preferred_element_type=jnp.float32)
    dst_rows = jnp.dot(feat_table, w_dst, preferred_element_type=jnp.float32)
    block_rows = min(128, atom_count)
    block_count = atom_count // block_rows
    pair_list = neighbors[0, 0]
    live_counts = counts[0, 0]

    def one_block(start_row):
        partner = lax.dynamic_slice_in_dim(pair_list, start_row, block_rows, 0)
        slot_count = lax.dynamic_slice_in_dim(live_counts, start_row, block_rows, 0)
        centre_geom = lax.dynamic_slice_in_dim(own_geom, start_row, block_rows, 1)
        part_geom = geo_table[:, partner]
        cell_shift = wrap_cells(
            part_geom[0:3].astype(jnp.int32) - centre_geom[0:3].astype(jnp.int32)[:, :, None], GRID
        ).astype(jnp.float32)
        displace = cell_shift + (part_geom[3:6] - centre_geom[3:6][:, :, None])
        live_slot = jnp.arange(partner.shape[1], dtype=jnp.int32)[None, :] < slot_count[:, None]
        return edge_update(
            lax.dynamic_slice_in_dim(own_rows, start_row, block_rows, 0),
            lax.dynamic_slice_in_dim(src_rows, start_row, block_rows, 0),
            dst_rows[partner],
            displace,
            live_slot,
            w_rad,
            w_mid,
            w_out,
        )

    start_rows = jnp.arange(block_count, dtype=jnp.int32) * block_rows
    new_rows = lax.map(one_block, start_rows).reshape(atom_count, channels)
    slab_x = GRID // dom_count
    slab_y = GRID // sub_count
    anchor_x = lax.axis_index("dom") * slab_x
    anchor_y = lax.axis_index("sub") * slab_y
    cells_x = anchor_x + jnp.arange(slab_x, dtype=jnp.int32)
    cells_y = anchor_y + jnp.arange(slab_y, dtype=jnp.int32)
    cells_z = jnp.arange(GRID, dtype=jnp.int32)
    charge_grid = jnp.zeros((GRID, slab_x * slab_y), jnp.float32)
    for place_x in range(3):
        for place_y in range(3):
            halo_geom = geo_halo[:, place_x, place_y]
            cell_rows = halo_geom[0:3].astype(jnp.int32)
            weight_x = axis_weights(cells_x, cell_rows[0], halo_geom[3])
            weight_y = axis_weights(cells_y, cell_rows[1], halo_geom[4])
            weight_z = axis_weights(cells_z, cell_rows[2], halo_geom[5])
            weight_plane = (
                weight_x[:, None, :] * weight_y[None, :, :] * halo_geom[6][None, None, :]
            ).reshape(slab_x * slab_y, atom_count)
            charge_grid = charge_grid + lax.dot_general(
                weight_z, weight_plane, (((1,), (1,)), ((), ())), precision=highest
            )
    charge_grid = charge_grid.reshape(GRID, slab_x, slab_y)
    cos_table, sin_table = dft_tables(GRID)
    spectrum = jnp.stack(
        [
            jnp.einsum("kz,zxy->kxy", cos_table, charge_grid, precision=highest),
            -jnp.einsum("kz,zxy->kxy", sin_table, charge_grid, precision=highest),
        ]
    )
    spectrum = swap_sub(spectrum)
    spectrum = complex_step(spectrum, cos_table, sin_table, "ky,zxy->kxz", 1.0)
    spectrum = swap_dom(spectrum)
    spectrum = complex_step(spectrum, cos_table, sin_table, "kx,yxz->kyz", 1.0)
    kx_ids = jnp.arange(GRID, dtype=jnp.int32)
    ky_ids = lax.axis_index("dom") * (GRID // dom_count) + jnp.arange(
        GRID // dom_count, dtype=jnp.int32
    )
    kz_ids = lax.axis_index("sub") * (GRID // sub_count) + jnp.arange(
        GRID // sub_count, dtype=jnp.int32
    )
    influence = influence_block(kx_ids, ky_ids, kz_ids) * (1.0 / GRID**3)
    spectrum = spectrum * influence[None]
    spectrum = complex_step(spectrum, cos_table, sin_table, "xk,kyz->xyz", -1.0)
    spectrum = swap_dom(spectrum)
    spectrum = complex_step(spectrum, cos_table, sin_table, "yk,xkz->yxz", -1.0)
    spectrum = swap_sub(spectrum)
    potential_grid = jnp.einsum(
        "zk,yxk->yxz", cos_table, spectrum[0], precision=highest
    ) - jnp.einsum("zk,yxk->yxz", sin_table, spectrum[1], precision=highest)
    potential_ext = extended(potential_grid, (("dom", 1), ("sub", 0)), 2)
    ext_x = anchor_x - 2 + jnp.arange(slab_x + 4, dtype=jnp.int32)
    ext_y = anchor_y - 2 + jnp.arange(slab_y + 4, dtype=jnp.int32)
    own_cells = offsets[:, 0, 0]
    own_frac = frac[:, 0, 0]
    weight_x = axis_weights(ext_x, own_cells[0], own_frac[0])
    weight_y = axis_weights(ext_y, own_cells[1], own_frac[1])
    weight_z = axis_weights(cells_z, own_cells[2], own_frac[2])
    along_z = jnp.dot(potential_ext.reshape(-1, GRID), weight_z, precision=highest)
    weight_xy = (weight_y[:, None, :] * weight_x[None, :, :]).reshape(-1, atom_count)
    potential = jnp.sum(weight_xy * along_z, axis=0)
    return (new_rows.reshape(1, 1, atom_count, channels), potential.reshape(1, 1, atom_count))


def solution(mesh):
    placed = (
        P("dom", "sub", None, None),
        P(None, "dom", "sub", None),
        P(None, "dom", "sub", None),
        P("dom", "sub", None, None),
        P("dom", "sub", None),
        P(),
        P(),
        P(),
        P(),
        P(),
        P(),
    )
    return jax.shard_map(
        local,
        mesh=mesh,
        in_specs=placed,
        out_specs=(P("dom", "sub", None, None), P("dom", "sub", None)),
        check_vma=False,
    )
```

profile of v0, /device:TPU:1, one launch (start us, length us, event | category | flops | bytes accessed | tf_op | source)
XLA Modules:
  0.0 895.9 jit_solution(9044082191898837386)
XLA Ops:
  7.3 7.8 collective-permute-start.1
  15.1 7.8 collective-permute-start.5
  40.3 8.3 collective-permute-done.3
  50.3 8.1 fusion.658
  162.3 11.7 %all-to-all-done.1 = f32[64,1,2048]{2,1,0:T(1,128)S(1)} async-done(((f32[64,1,2048]{2,1,0:T(1,128)}), f32[64,1,2048]{2,1,0:T(1,128)S(1)}, u32[]{:S(2)}, u32[]{:S(2)}) %all-to-all-start.1) | async-done | bytes 524320 | tf_op jit(solution)/shard_map/all_to_all | solution.py:137
  207.0 10.5 %all-to-all-done.2 = f32[64,1,2048]{2,1,0:T(1,128)S(1)} async-done(((f32[64,1,2048]{2,1,0:T(1,128)}), f32[64,1,2048]{2,1,0:T(1,128)S(1)}, u32[]{:S(2)}, u32[]{:S(2)}) %all-to-all-start.2) | async-done | bytes 524320 | tf_op jit(solution)/shard_map/all_to_all | solution.py:137
  268.3 617.1 %while.12 = (s32[]{:T(128)}, bf16[16,128,128]{2,1,0:T(8,128)(2,1)}, s32[16]{0:T(128)}, bf16[2048,128]{1,0:T(8,128)(2,1)}, s32[2048,16]{1,0:T(8,128)}, /*index=5*...) while((s32[]{:T(128)}, bf16[16,128,128]{2,1,0:T(8,128)(2,1)}, ...), condition=%wide.region_4.5_spmd, body=%wide.region_0.4_spmd.sunk | while | flops 137124224 | bytes 9598315 | solution.py:202
  272.5 9.5 %gather_fusion = f32[2048,6]{1,0:T(8,128)} fusion(f32[6,6144]{0,1:T(8,128)} %get-tuple-element.492, s32[2048]{0:T(1024)S(1)} %broadcast_clamp_fusion.2), kind=kCustom, calls=%fused_computation.clone.1 | custom fusion | bytes 106496 | tf_op jit(solution)/shard_map/while/body/eval_jaxpr/gather | solution.py:184
  284.8 7.6 gather_fusion.1
  311.1 9.5 %gather_fusion = f32[2048,6]{1,0:T(8,128)} fusion(f32[6,6144]{0,1:T(8,128)} %get-tuple-element.492, s32[2048]{0:T(1024)S(1)} %broadcast_clamp_fusion.2), kind=kCustom, calls=%fused_computation.clone.1 | custom fusion | bytes 106496 | tf_op jit(solution)/shard_map/while/body/eval_jaxpr/gather | solution.py:184
  323.3 7.6 gather_fusion.1
  349.7 9.5 %gather_fusion = f32[2048,6]{1,0:T(8,128)} fusion(f32[6,6144]{0,1:T(8,128)} %get-tuple-element.492, s32[2048]{0:T(1024)S(1)} %broadcast_clamp_fusion.2), kind=kCustom, calls=%fused_computation.clone.1 | custom fusion | bytes 106496 | tf_op jit(solution)/shard_map/while/body/eval_jaxpr/gather | solution.py:184
  361.9 7.6 gather_fusion.1
  388.3 9.5 %gather_fusion = f32[2048,6]{1,0:T(8,128)} fusion(f32[6,6144]{0,1:T(8,128)} %get-tuple-element.492, s32[2048]{0:T(1024)S(1)} %broadcast_clamp_fusion.2), kind=kCustom, calls=%fused_computation.clone.1 | custom fusion | bytes 106496 | tf_op jit(solution)/shard_map/while/body/eval_jaxpr/gather | solution.py:184
  400.5 7.6 gather_fusion.1
  426.8 9.5 %gather_fusion = f32[2048,6]{1,0:T(8,128)} fusion(f32[6,6144]{0,1:T(8,128)} %get-tuple-element.492, s32[2048]{0:T(1024)S(1)} %broadcast_clamp_fusion.2), kind=kCustom, calls=%fused_computation.clone.1 | custom fusion | bytes 106496 | tf_op jit(solution)/shard_map/while/body/eval_jaxpr/gather | solution.py:184
  439.1 7.6 gather_fusion.1
  465.4 9.5 %gather_fusion = f32[2048,6]{1,0:T(8,128)} fusion(f32[6,6144]{0,1:T(8,128)} %get-tuple-element.492, s32[2048]{0:T(1024)S(1)} %broadcast_clamp_fusion.2), kind=kCustom, calls=%fused_computation.clone.1 | custom fusion | bytes 106496 | tf_op jit(solution)/shard_map/while/body/eval_jaxpr/gather | solution.py:184
  477.7 7.6 gather_fusion.1
  504.0 9.5 %gather_fusion = f32[2048,6]{1,0:T(8,128)} fusion(f32[6,6144]{0,1:T(8,128)} %get-tuple-element.492, s32[2048]{0:T(1024)S(1)} %broadcast_clamp_fusion.2), kind=kCustom, calls=%fused_computation.clone.1 | custom fusion | bytes 106496 | tf_op jit(solution)/shard_map/while/body/eval_jaxpr/gather | solution.py:184
  516.2 7.6 gather_fusion.1
  542.6 9.5 %gather_fusion = f32[2048,6]{1,0:T(8,128)} fusion(f32[6,6144]{0,1:T(8,128)} %get-tuple-element.492, s32[2048]{0:T(1024)S(1)} %broadcast_clamp_fusion.2), kind=kCustom, calls=%fused_computation.clone.1 | custom fusion | bytes 106496 | tf_op jit(solution)/shard_map/while/body/eval_jaxpr/gather | solution.py:184
  554.8 7.6 gather_fusion.1
  581.2 9.5 %gather_fusion = f32[2048,6]{1,0:T(8,128)} fusion(f32[6,6144]{0,1:T(8,128)} %get-tuple-element.492, s32[2048]{0:T(1024)S(1)} %broadcast_clamp_fusion.2), kind=kCustom, calls=%fused_computation.clone.1 | custom fusion | bytes 106496 | tf_op jit(solution)/shard_map/while/body/eval_jaxpr/gather | solution.py:184
  619.7 9.5 %gather_fusion = f32[2048,6]{1,0:T(8,128)} fusion(f32[6,6144]{0,1:T(8,128)} %get-tuple-element.492, s32[2048]{0:T(1024)S(1)} %broadcast_clamp_fusion.2), kind=kCustom, calls=%fused_computation.clone.1 | custom fusion | bytes 106496 | tf_op jit(solution)/shard_map/while/body/eval_jaxpr/gather | solution.py:184
  658.3 9.5 %gather_fusion = f32[2048,6]{1,0:T(8,128)} fusion(f32[6,6144]{0,1:T(8,128)} %get-tuple-element.492, s32[2048]{0:T(1024)S(1)} %broadcast_clamp_fusion.2), kind=kCustom, calls=%fused_computation.clone.1 | custom fusion | bytes 106496 | tf_op jit(solution)/shard_map/while/body/eval_jaxpr/gather | solution.py:184
  696.9 9.5 %gather_fusion = f32[2048,6]{1,0:T(8,128)} fusion(f32[6,6144]{0,1:T(8,128)} %get-tuple-element.492, s32[2048]{0:T(1024)S(1)} %broadcast_clamp_fusion.2), kind=kCustom, calls=%fused_computation.clone.1 | custom fusion | bytes 106496 | tf_op jit(solution)/shard_map/while/body/eval_jaxpr/gather | solution.py:184
  735.4 9.5 %gather_fusion = f32[2048,6]{1,0:T(8,128)} fusion(f32[6,6144]{0,1:T(8,128)} %get-tuple-element.492, s32[2048]{0:T(1024)S(1)} %broadcast_clamp_fusion.2), kind=kCustom, calls=%fused_computation.clone.1 | custom fusion | bytes 106496 | tf_op jit(solution)/shard_map/while/body/eval_jaxpr/gather | solution.py:184
  774.0 9.5 %gather_fusion = f32[2048,6]{1,0:T(8,128)} fusion(f32[6,6144]{0,1:T(8,128)} %get-tuple-element.492, s32[2048]{0:T(1024)S(1)} %broadcast_clamp_fusion.2), kind=kCustom, calls=%fused_computation.clone.1 | custom fusion | bytes 106496 | tf_op jit(solution)/shard_map/while/body/eval_jaxpr/gather | solution.py:184
  812.6 9.5 %gather_fusion = f32[2048,6]{1,0:T(8,128)} fusion(f32[6,6144]{0,1:T(8,128)} %get-tuple-element.492, s32[2048]{0:T(1024)S(1)} %broadcast_clamp_fusion.2), kind=kCustom, calls=%fused_computation.clone.1 | custom fusion | bytes 106496 | tf_op jit(solution)/shard_map/while/body/eval_jaxpr/gather | solution.py:184
  851.1 9.5 %gather_fusion = f32[2048,6]{1,0:T(8,128)} fusion(f32[6,6144]{0,1:T(8,128)} %get-tuple-element.492, s32[2048]{0:T(1024)S(1)} %broadcast_clamp_fusion.2), kind=kCustom, calls=%fused_computation.clone.1 | custom fusion | bytes 106496 | tf_op jit(solution)/shard_map/while/body/eval_jaxpr/gather | solution.py:184
  886.5 9.2 %fusion.27 = f32[2048]{0:T(1024)} fusion(f32[8,2048]{1,0:T(8,128)} %fusion.857, f32[68,2048]{1,0:T(8,128)} %fusion.608, s32[2048]{0:T(1024)} %bitcast.459, f32[2048]{0:T(1024)S(1)} %bitcast.458, f32[68,8,256]{2,0,1:T(8,128)S(1)} %pad_maximum_fusion), kind=kOutput, calls=%fused_computation.66 | convolution fusion | flops 3451582464 | bytes 1204224 | tf_op jit(solution)/shard_map/dot_general | solution.py:260
  (901 shorter events, 585.0 us)
Async XLA Ops:
  0.6 259.3 %copy-start = (bf16[128,128]{1,0:T(8,128)(2,1)S(1)}, bf16[128,128]{1,0:T(8,128)(2,1)}, u32[]{:S(2)}) copy-start(bf16[128,128]{1,0:T(8,128)(2,1)} %param.19) | copy-start | bytes 98308
  0.6 14.4 %copy-start.1 = (bf16[1,1,2048,128]{3,2,1,0:T(8,128)(2,1)S(1)}, bf16[1,1,2048,128]{3,2,1,0:T(8,128)(2,1)}, u32[]{:S(2)}) copy-start(bf16[1,1,2048,128]{3,2,1,0:T(8,128)(2,1)} %param.13) | copy-start | bytes 1572868
  2.3 23.9 %copy-start.13 = (s32[1,1,2048,16]{2,3,1,0:T(8,128)S(1)}, s32[1,1,2048,16]{2,3,1,0:T(8,128)}, u32[]{:S(2)}) copy-start(s32[1,1,2048,16]{2,3,1,0:T(8,128)} %param.16) | copy-start | bytes 393220
  2.9 24.7 %copy-start.16 = (bf16[128,128]{1,0:T(8,128)(2,1)S(1)}, bf16[128,128]{1,0:T(8,128)(2,1)}, u32[]{:S(2)}) copy-start(bf16[128,128]{1,0:T(8,128)(2,1)} %param.18) | copy-start | bytes 98308
  3.4 29.1 %collective-permute-start = (f32[7,1,1,2048]{3,2,1,0:T(1,128)S(1)}, f32[7,1,1,2048]{3,2,1,0:T(1,128)S(1)}, u32[]{:S(2)}, u32[]{:S(2)}) collective-permute-start(f32[7,1,1,2048]{3,2,1,0:T(1,128)S(1)} %pad_maximum_fusion.6), channel_id=1, source_target_pairs={{0,4},{4,8},{8,12},{12,16},{16,20},{20,24},{24,28},{28,32},{32,36}... | collective-permute-start | bytes 172040 | tf_op jit(solution)/shard_map/ppermute | solution.py:24
  7.3 25.2 %collective-permute-start.1 = (f32[7,1,1,2048]{3,2,1,0:T(1,128)S(1)}, f32[7,1,1,2048]{3,2,1,0:T(1,128)S(1)}, u32[]{:S(2)}, u32[]{:S(2)}) collective-permute-start(f32[7,1,1,2048]{3,2,1,0:T(1,128)S(1)} %pad_maximum_fusion.6), channel_id=1, source_target_pairs={{4,0},{8,4},{12,8},{16,12},{20,16},{24,20},{28,24},{32,28},{36,32}... | collective-permute-start | bytes 172040 | tf_op jit(solution)/shard_map/ppermute | solution.py:25
  15.1 141.3 %collective-permute-start.4 = (bf16[1,1,2048,128]{3,2,1,0:T(8,128)(2,1)S(1)}, bf16[1,1,2048,128]{3,2,1,0:T(8,128)(2,1)}, u32[]{:S(2)}, u32[]{:S(2)}) collective-permute-start(bf16[1,1,2048,128]{3,2,1,0:T(8,128)(2,1)S(1)} %copy-done.1), channel_id=1, source_target_pairs={{0,4},{4,8},{8,12},{12,16},{16,20},{20,24},{24,28},{28,32},{32,36}... | collective-permute-start | bytes 1572872 | tf_op jit(solution)/shard_map/ppermute | solution.py:24
  15.1 144.0 %collective-permute-start.5 = (bf16[1,1,2048,128]{3,2,1,0:T(8,128)(2,1)S(1)}, bf16[1,1,2048,128]{3,2,1,0:T(8,128)(2,1)}, u32[]{:S(2)}, u32[]{:S(2)}) collective-permute-start(bf16[1,1,2048,128]{3,2,1,0:T(8,128)(2,1)S(1)} %copy-done.1), channel_id=1, source_target_pairs={{4,0},{8,4},{12,8},{16,12},{20,16},{24,20},{28,24},{32,28},{36,32}... | collective-permute-start | bytes 1572872 | tf_op jit(solution)/shard_map/ppermute | solution.py:25
  32.7 7.6 collective-permute-start.2
  34.9 13.7 %collective-permute-start.3 = (f32[7,3,1,2048]{3,2,1,0:T(1,128)S(1)}, f32[7,3,1,2048]{3,2,1,0:T(1,128)S(1)}, u32[]{:S(2)}, u32[]{:S(2)}) collective-permute-start(f32[7,3,1,2048]{3,2,1,0:T(1,128)S(1)} %pad_maximum_fusion.5), channel_id=1, source_target_pairs={{1,0},{2,1},{3,2},{0,3},{5,4},{6,5},{7,6},{4,7},{9,8},{10,9},{11,1... | collective-permute-start | bytes 516104 | tf_op jit(solution)/shard_map/ppermute | solution.py:25
  40.2 18.2 %copy-start.12 = (f32[7,3,1,2048]{3,2,1,0:T(1,128)}, f32[7,3,1,2048]{3,2,1,0:T(1,128)S(1)}, u32[]{:S(2)}) copy-start(f32[7,3,1,2048]{3,2,1,0:T(1,128)S(1)} %collective-permute-done.2) | copy-start | bytes 516100
  48.6 9.9 %copy-start.11 = (f32[7,3,1,2048]{3,2,1,0:T(1,128)}, f32[7,3,1,2048]{3,2,1,0:T(1,128)S(1)}, u32[]{:S(2)}) copy-start(f32[7,3,1,2048]{3,2,1,0:T(1,128)S(1)} %collective-permute-done.3) | copy-start | bytes 516100
  119.2 10.9 %all-to-all-start = ((f32[4,1,32768]{2,1,0:T(1,128)}), f32[4,1,32768]{2,1,0:T(1,128)S(1)}, u32[]{:S(2)}, u32[]{:S(2)}) async-start(f32[4,1,32768]{2,1,0:T(1,128)} %reshape.2312), calls=%async_computation | async-start | bytes 1048576 | tf_op jit(solution)/shard_map/all_to_all | solution.py:133
  146.5 9.3 %copy-start.15 = (f32[6,1,1,512]{3,2,1,0:T(1,128)S(1)}, f32[6,1,1,512]{3,2,1,0:T(1,128)}, u32[]{:S(2)}) copy-start(f32[6,1,1,512]{3,2,1,0:T(1,128)} %slice.667) | copy-start | bytes 36868
  149.8 24.2 %all-to-all-start.1 = ((f32[64,1,2048]{2,1,0:T(1,128)}), f32[64,1,2048]{2,1,0:T(1,128)S(1)}, u32[]{:S(2)}, u32[]{:S(2)}) async-start(f32[64,1,2048]{2,1,0:T(1,128)} %reshape.2314), calls=%async_computation.1 | async-start | bytes 1048576 | tf_op jit(solution)/shard_map/all_to_all | solution.py:137
  161.0 42.3 %collective-permute-start.6 = (bf16[3,1,2048,128]{3,2,1,0:T(8,128)(2,1)}, bf16[3,1,2048,128]{3,2,1,0:T(8,128)(2,1)}, u32[]{:S(2)}, u32[]{:S(2)}) collective-permute-start(bf16[3,1,2048,128]{3,2,1,0:T(8,128)(2,1)} %constant_dynamic-update-slice_fusion.18), channel_id=1, source_target_pairs={{0,1},{1,2},{2,3},{3,0},{4,5},{5,6},{6,7},{7,4},{8,9},{9,10},{10,1... | collective-permute-start | bytes 4718600 | tf_op jit(solution)/shard_map/ppermute | solution.py:24
  162.2 43.0 %collective-permute-start.7 = (bf16[3,1,2048,128]{3,2,1,0:T(8,128)(2,1)}, bf16[3,1,2048,128]{3,2,1,0:T(8,128)(2,1)}, u32[]{:S(2)}, u32[]{:S(2)}) collective-permute-start(bf16[3,1,2048,128]{3,2,1,0:T(8,128)(2,1)} %constant_dynamic-update-slice_fusion.18), channel_id=1, source_target_pairs={{1,0},{2,1},{3,2},{0,3},{5,4},{6,5},{7,6},{4,7},{9,8},{10,9},{11,1... | collective-permute-start | bytes 4718600 | tf_op jit(solution)/shard_map/ppermute | solution.py:25
  195.4 22.2 %all-to-all-start.2 = ((f32[64,1,2048]{2,1,0:T(1,128)}), f32[64,1,2048]{2,1,0:T(1,128)S(1)}, u32[]{:S(2)}, u32[]{:S(2)}) async-start(f32[64,1,2048]{2,1,0:T(1,128)} %reshape.2316), calls=%async_computation.2 | async-start | bytes 1048576 | tf_op jit(solution)/shard_map/all_to_all | solution.py:137
  229.5 15.5 %all-to-all-start.3 = ((f32[4,1,32768]{2,1,0:T(1,128)}), f32[4,1,32768]{2,1,0:T(1,128)S(1)}, u32[]{:S(2)}, u32[]{:S(2)}) async-start(f32[4,1,32768]{2,1,0:T(1,128)} %reshape.2318), calls=%async_computation.3 | async-start | bytes 1048576 | tf_op jit(solution)/shard_map/all_to_all | solution.py:133
  252.0 10.7 %copy-start.3 = (f32[64,4,256]{2,0,1:T(8,128)}, f32[64,4,256]{2,0,1:T(8,128)S(1)}, u32[]{:S(2)}) copy-start(f32[64,4,256]{2,0,1:T(8,128)S(1)} %convolution_subtract_fusion) | copy-start | bytes 786436
  252.1 10.6 %collective-permute-start.8 = (f32[64,2,256]{2,0,1:T(8,128)S(1)}, f32[64,2,256]{2,0,1:T(8,128)S(1)}, u32[]{:S(2)}, u32[]{:S(2)}) collective-permute-start(f32[64,2,256]{2,0,1:T(8,128)S(1)} %get-tuple-element.253), channel_id=1, source_target_pairs={{0,4},{4,8},{8,12},{12,16},{16,20},{20,24},{24,28},{28,32},{32,36}... | collective-permute-start | bytes 393224 | tf_op jit(solution)/shard_map/ppermute | solution.py:24
  253.8 8.9 collective-permute-start.9
  263.4 622.0 %collective-permute-start.10 = (f32[2,8,256]{2,0,1:T(2,128)}, f32[2,8,256]{2,0,1:T(2,128)}, u32[]{:S(2)}, u32[]{:S(2)}) collective-permute-start(f32[2,8,256]{2,0,1:T(2,128)} %get-tuple-element.249), channel_id=1, source_target_pairs={{0,1},{1,2},{2,3},{3,0},{4,5},{5,6},{6,7},{7,4},{8,9},{9,10},{10,1... | collective-permute-start | bytes 49160 | tf_op jit(solution)/shard_map/ppermute | solution.py:24
  268.1 617.3 %collective-permute-start.11 = (f32[2,8,256]{2,0,1:T(2,128)}, f32[2,8,256]{2,0,1:T(2,128)}, u32[]{:S(2)}, u32[]{:S(2)}) collective-permute-start(f32[2,8,256]{2,0,1:T(2,128)} %get-tuple-element.250), channel_id=1, source_target_pairs={{1,0},{2,1},{3,2},{0,3},{5,4},{6,5},{7,6},{4,7},{9,8},{10,9},{11,1... | collective-permute-start | bytes 49160 | tf_op jit(solution)/shard_map/ppermute | solution.py:25
  400.5 8.5 copy-start.20
  439.1 8.5 copy-start.20
  477.7 8.5 copy-start.20
  516.2 8.5 copy-start.20
  554.8 8.5 copy-start.20
  593.4 8.5 copy-start.20
  631.9 8.5 copy-start.20
  670.5 8.5 copy-start.20
  (50 other events, 231.8 us)
where the time goes:
time: 910 us; the launch traced here: 896 us
  local copies, waits for them, and re-layouts  425 us (47%)
  matrix products  279 us (31%)
  starting transfers between devices  58.7 us (6%)
  other arithmetic  57 us (6%)
  waiting for transfers between devices  40.9 us (4%)
  loops' own time  33.4 us (4%)
    gather x32, local copies, waits for them, and re-layouts, one_block(): part_geom = geo_table[:, partner]  178 us
    gather x16, local copies, waits for them, and re-layouts, one_block(): dst_rows[partner]  122 us
    dot_general x16, matrix products, edge_update(): radial_term = jnp.einsum('akn,nc->akc', radial, w_rad, precision=highest)  66.2 us
    dot_general x16, matrix products, edge_update(): moments = jnp.einsum('akc,mak->amc', message, angular, precision=highest)  52.2 us
    dot_general x9, matrix products, local(): lax.dot_general(weight_z, weight_plane, (((1,), (1,)), ((), ())), precisi...  48.9 us
    dot_general x16, matrix products, edge_update(): jnp.einsum('akc,cd->akd', latent, w_mid, preferred_element_type=jnp.float32)  39.9 us
    another operation x1, loops' own time, local(): new_rows = lax.map(one_block, start_rows).reshape(atom_count, channels)  33.4 us
    unnamed x64, local copies, waits for them, and re-layouts  28.6 us
  transfers between devices with their start and end apart: 16, of which 7 were waited for; matrix products, arithmetic and copies ran while one was open for 81% of the time, Pallas kernels for 0%

commit v1 on v0

v1 whole, which is shorter than its diff:
```python
import functools
import math

import jax
import jax.numpy as jnp
import ml_dtypes
import numpy as np
from jax import lax
from jax.experimental import pallas as pl
from jax.experimental.pallas import tpu as pltpu
from jax.sharding import PartitionSpec as P

GRID = 256
ext_x = 7
ext_y = 67
rows_y = 72
head_rows = 512
table_pad = 8
halo_places = [(0, 0), (0, 1), (0, 2), (1, 0), (1, 2), (2, 0), (2, 1), (2, 2)]


def split_table(table):
    high = table.astype(ml_dtypes.bfloat16)
    low = (table - high.astype(np.float64)).astype(ml_dtypes.bfloat16)
    return high, low


def real_basis():
    cells = np.arange(GRID)
    basis = np.zeros((GRID, GRID))
    for k in range(GRID):
        wave = k if k <= GRID // 2 else k - GRID // 2
        angle = 2.0 * np.pi / GRID * ((wave * cells) % GRID)
        scale = math.sqrt((1.0 if k in (0, GRID // 2) else 2.0) / GRID)
        basis[k] = scale * (np.cos(angle) if k <= GRID // 2 else np.sin(angle))
    return basis


def wave_tables():
    index = np.arange(GRID)
    wave = np.where(index <= GRID // 2, index, index - GRID // 2) / GRID
    factor = (2.0 + np.cos(2.0 * np.pi * wave)) / 3.0
    return (wave**2).astype(np.float32), (1.0 / factor**2).astype(np.float32)


basis = real_basis()
columns_y = np.zeros((GRID, 4 * rows_y))
for c in range(4):
    for y in range(ext_y):
        columns_y[:, c * rows_y + y] = basis[:, (64 * c - 1 + y) % GRID]
columns_x = np.concatenate([basis[:, (4 * np.arange(64) - 1 + x) % GRID] for x in range(ext_x)], axis=1)
forward_z = split_table(basis.T.copy())
inverse_z = split_table(basis)
forward_y = split_table(columns_y)
inverse_y = split_table(columns_y.T.copy())
forward_x = split_table(columns_x)
inverse_x = split_table(columns_x.T.copy())
wave_square, wave_factor = wave_tables()

VMEM = pl.BlockSpec(memory_space=pltpu.VMEM)
SMEM = pl.BlockSpec(memory_space=pltpu.SMEM)
ANY = pl.BlockSpec(memory_space=pl.ANY)


def kernel_call(body, out_shape, in_specs, scratch=(), name=None, flops=0, moved=0):
    return pl.pallas_call(
        body,
        in_specs=in_specs,
        out_specs=jax.tree.map(lambda _: VMEM, out_shape),
        out_shape=out_shape,
        scratch_shapes=list(scratch),
        compiler_params=pltpu.CompilerParams(vmem_limit_bytes=40 * 2**20),
        cost_estimate=pl.CostEstimate(flops=flops, bytes_accessed=moved, transcendentals=0),
        name=name,
    )


def halves(x):
    high = x.astype(jnp.bfloat16)
    return high, (x - high.astype(jnp.float32)).astype(jnp.bfloat16)


def dot_split(a, b, pattern=(((1,), (0,)), ((), ()))):
    dot = functools.partial(lax.dot_general, dimension_numbers=pattern, preferred_element_type=jnp.float32)
    return dot(a[0], b[0]) + (dot(a[0], b[1]) + dot(a[1], b[0]))


def spline_four(f):
    g = 1.0 - f
    f2 = f * f
    f3 = f2 * f
    return (
        g * g * g * (1.0 / 6.0),
        (3.0 * f3 - 6.0 * f2 + 4.0) * (1.0 / 6.0),
        (-3.0 * f3 + 3.0 * f2 + 3.0 * f + 1.0) * (1.0 / 6.0),
        f3 * (1.0 / 6.0),
    )


def placed_weights(count, cell, f, wraps=False):
    ids = lax.broadcasted_iota(jnp.int32, (count, cell.shape[1]), 0)
    step = ids - cell
    if wraps:
        step = (step + 1) & (GRID - 1)
    result = jnp.zeros(step.shape, jnp.float32)
    for k, weight in enumerate(spline_four(f)):
        result = jnp.where(step == k, weight, result)
    return result


def pair_tiles(first, second, half):
    lane = lax.broadcasted_iota(jnp.int32, first.shape, 1)
    if half == 0:
        return jnp.where(lane < 64, first, pltpu.roll(second, 64, 1))
    return jnp.where(lane < 64, pltpu.roll(first, 64, 1), second)


def spread_kernel(cell_ref, frac_ref, feat_ref, w_ref, thi_ref, tlo_ref, out_ref, grid_s, charge_s):
    f32, bf16 = jnp.float32, jnp.bfloat16
    w = jnp.broadcast_to(w_ref[...], (16, 128))
    top = w.astype(bf16).astype(f32)
    mid = (w - top).astype(bf16).astype(f32)
    sub = lax.broadcasted_iota(jnp.int32, (16, 128), 0)
    parts = jnp.where(sub == 0, top, jnp.where(sub == 1, mid, jnp.where(sub == 2, w - top - mid, 0.0))).astype(bf16)
    raw = lax.dot_general(parts, feat_ref[...], (((1,), (1,)), ((), ())), preferred_element_type=f32)
    raw = jnp.broadcast_to(raw[0:1] + raw[1:2] + raw[2:3], (8, raw.shape[1]))
    atoms = raw.shape[1]
    lane = lax.broadcasted_iota(jnp.int32, raw.shape, 1)
    mate = jnp.where(lane % 2 == 0, pltpu.roll(raw, atoms - 1, 1), pltpu.roll(raw, 1, 1))
    charge_s[...] = 0.5 * (raw - mate)
    grid_s[...] = jnp.zeros_like(grid_s)

    def tile(i, carry):
        cols = pl.ds(pl.multiple_of(i * 512, 512), 512)
        along_x = placed_weights(8, cell_ref[0:1, cols], frac_ref[0:1, cols]) * charge_s[0:1, cols]
        along_y = placed_weights(rows_y, cell_ref[1:2, cols], frac_ref[1:2, cols])
        along_z = placed_weights(GRID, cell_ref[2:3, cols], frac_ref[2:3, cols], True)
        plane = jnp.concatenate([along_x[x : x + 1] * along_y for x in range(ext_x)], axis=0)
        grid_s[...] += dot_split(halves(plane), halves(along_z), (((1,), (1,)), ((), ())))
        return carry

    lax.fori_loop(0, atoms // 512, tile, 0)
    waves = dot_split(halves(grid_s[...]), (thi_ref[...], tlo_ref[...]))
    for q in range(4):
        for c in range(4):
            cols = slice(128 * (c // 2), 128 * (c // 2) + 128)
            first = waves[2 * q * rows_y : (2 * q + 1) * rows_y, cols]
            if 2 * q + 1 < ext_x:
                second = waves[(2 * q + 1) * rows_y : (2 * q + 2) * rows_y, cols]
            else:
                second = jnp.zeros_like(first)
            out_ref[c, :, q * 128 : q * 128 + 128] = pair_tiles(first, second, c % 2)


def forward_y_kernel(x_ref, thi_ref, tlo_ref, after_ref, out_ref):
    data = jnp.concatenate([x_ref[c] for c in range(4)], axis=0)
    waves = dot_split((thi_ref[...], tlo_ref[...]), halves(data))
    for j in range(4):
        out_ref[:, 0, j * 512 : j * 512 + 512] = waves[64 * j : 64 * j + 64]


def filter_kernel(x_ref, thi_ref, tlo_ref, uhi_ref, ulo_ref, col_ref, row_ref, after_ref, out_ref):
    slabs = [x_ref[:, 0, j * 512 : j * 512 + 512] for j in range(4)]
    pieces = []
    for x in range(ext_x):
        cols = slice(128 * (x // 2), 128 * (x // 2) + 128)
        pieces.append(
            jnp.concatenate(
                [pair_tiles(slabs[2 * p][:, cols], slabs[2 * p + 1][:, cols], x % 2) for p in range(2)], axis=1
            )
        )
    waves = dot_split((thi_ref[...], tlo_ref[...]), halves(jnp.concatenate(pieces, axis=0)))
    square = col_ref[0] + row_ref[0:1, :]
    factor = col_ref[1] * row_ref[1:2, :]
    positive = square > 0.0
    safe = jnp.where(positive, square, 1.0)
    influence = jnp.where(positive, 16.0 * jnp.exp(square * (-(math.pi**2))) / safe * factor, 0.0)
    cells = dot_split((uhi_ref[...], ulo_ref[...]), halves(waves * influence))
    for j in range(4):
        for q in range(4):
            cols = slice(128 * (j // 2), 128 * (j // 2) + 128)
            first = cells[128 * q : 128 * q + 64, cols]
            if 2 * q + 1 < ext_x:
                second = cells[128 * q + 64 : 128 * q + 128, cols]
            else:
                second = jnp.zeros_like(first)
            out_ref[:, 0, j * 512 + q * 128 : j * 512 + q * 128 + 128] = pair_tiles(first, second, j % 2)


def inverse_y_kernel(x_ref, thi_ref, tlo_ref, after_ref, out_ref):
    data = jnp.concatenate([x_ref[:, 0, j * 512 : j * 512 + 512] for j in range(4)], axis=0)
    cells = dot_split((thi_ref[...], tlo_ref[...]), halves(data))
    for c in range(4):
        out_ref[c] = cells[c * rows_y : (c + 1) * rows_y]


def read_kernel(x_ref, cell_ref, frac_ref, thi_ref, tlo_ref, after_ref, out_ref, grid_s):
    pieces = []
    for x in range(ext_x):
        cols = slice(128 * (x // 2), 128 * (x // 2) + 128)
        pieces.append(
            jnp.concatenate(
                [pair_tiles(x_ref[2 * p, :, cols], x_ref[2 * p + 1, :, cols], x % 2) for p in range(2)], axis=1
            )
        )
    grid_s[...] = dot_split(halves(jnp.concatenate(pieces, axis=0)), (thi_ref[...], tlo_ref[...]))

    def tile(i, carry):
        cols = pl.ds(pl.multiple_of(i * 512, 512), 512)
        along_x = placed_weights(8, cell_ref[0:1, cols], frac_ref[0:1, cols])
        along_y = placed_weights(rows_y, cell_ref[1:2, cols], frac_ref[1:2, cols])
        along_z = placed_weights(GRID, cell_ref[2:3, cols], frac_ref[2:3, cols], True)
        lines = dot_split(halves(grid_s[...]), halves(along_z))
        total = jnp.zeros(along_y.shape, jnp.float32)
        for x in range(ext_x):
            total = total + along_x[x : x + 1] * lines[x * rows_y : (x + 1) * rows_y]
        out_ref[:, cols] = jnp.sum(total * along_y, axis=0, keepdims=True)
        return carry

    lax.fori_loop(0, out_ref.shape[1] // 512, tile, 0)


def tables_kernel(own_ref, mid_ref, left_ref, right_ref, cell_ref, wsrc_ref, wdst_ref, tab_ref, src_ref, geo_ref):
    f32 = jnp.float32
    half = lambda ref: (ref[...].astype(f32) * 0.5).astype(jnp.bfloat16)
    w_src, w_dst = half(wsrc_ref), half(wdst_ref)
    own = own_ref[...]
    src_ref[...] = jnp.dot(own, w_src, preferred_element_type=f32)
    tab_ref[table_pad : table_pad + 2048, :] = jnp.dot(own, w_dst, preferred_element_type=f32)
    tab_ref[0:table_pad, :] = jnp.zeros((table_pad, 128), f32)
    tab_ref[table_pad + 6144 :, :] = jnp.zeros((table_pad, 128), f32)
    for c in range(3):
        geo_ref[c * 48 : c * 48 + 16, :] = cell_ref[c * 16 : c * 16 + 16, :]
    for r, (place_x, place_y) in enumerate(halo_places):
        ref = {0: left_ref, 1: mid_ref, 2: right_ref}[place_y]
        row = place_x if place_y != 1 else place_x // 2
        base = table_pad + 2048 + r * head_rows
        tab_ref[base : base + head_rows, :] = jnp.dot(ref[row, 0:head_rows, :], w_dst, preferred_element_type=f32)
        tail = ref[row, head_rows : head_rows + 48, :].astype(f32)
        for c in range(3):
            value = sum(tail[s * 12 + c * 4 : s * 12 + c * 4 + 4] for s in range(3))
            shift = (4.0 * (place_x - 1), 64.0 * (place_y - 1), 0.0)[c]
            geo_ref[c * 48 + 16 + r * 4 : c * 48 + 16 + r * 4 + 4, :] = value + shift


def edge_kernel(idx_ref, nb_ref, geo_ref, cnt_ref, tab_ref, src_ref, own_ref, wrad_ref, wmid_ref, wout_ref, after_ref, out_ref, ang_s, rad_s, inv_s, *, start, blocks):
    f32, bf16 = jnp.float32, jnp.bfloat16
    sub = lax.broadcasted_iota(jnp.int32, (8, 128), 0)
    lane = lax.broadcasted_iota(jnp.int32, (8, 128), 1)
    wr = wrad_ref[...] * 0.5
    wr_hi = wr.astype(bf16).astype(f32)
    w_ext = jnp.concatenate([wr_hi, wr_hi, wr - wr_hi, jnp.zeros_like(wr)], axis=0).astype(bf16)
    w_mid = (wmid_ref[...].astype(f32) * 0.5).astype(bf16)
    diag = (lane // 16) == sub

    def body(i, carry):
        g = start + i
        rows = pl.ds(pl.multiple_of(g * 8, 8), 8)
        nb = nb_ref[rows, :]
        low = nb & 127
        high = nb >> 7
        part = [jnp.zeros((8, 128), f32) for _ in range(3)]
        for h in range(48):
            hit = high == h
            for c in range(3):
                row = jnp.broadcast_to(geo_ref[c * 48 + h : c * 48 + h + 1, :], (8, 128))
                part[c] = jnp.where(hit, jnp.take_along_axis(row, low, axis=1), part[c])
        centre_lane = (g % 2) * 64 + sub * 8 + lane // 16
        mine = [
            jnp.take_along_axis(
                jnp.broadcast_to(geo_ref[pl.ds(c * 48 + g // 2, 1), :], (8, 128)), centre_lane, axis=1
            )
            for c in range(3)
        ]
        live = jnp.take_along_axis(
            jnp.broadcast_to(cnt_ref[pl.ds(g // 2, 1), :], (8, 128)), centre_lane, axis=1
        )
        dx = part[0] - mine[0]
        dy = part[1] - mine[1]
        dz = part[2] - mine[2]
        cells = jnp.floor(part[2]) - jnp.floor(mine[2])
        dz = jnp.where(cells >= 128.0, dz - 256.0, jnp.where(cells < -128.0, dz + 256.0, dz))
        squared = dx * dx + dy * dy + dz * dz + 1.0
        distance = jnp.sqrt(squared)
        inverse = 1.0 / distance
        nx, ny, nz = dx * inverse, dy * inverse, dz * inverse
        env = jnp.where((lane % 16) < live, 1.0 / (1.0 + squared * (1.0 / 4096.0)), 0.0)
        r3, r5, r15 = math.sqrt(3.0), math.sqrt(5.0), math.sqrt(15.0)
        ex, ey, ez = env * nx, env * ny, env * nz
        angular = [
            env, r3 * ex, r3 * ey, r3 * ez, r15 * ex * ny, r15 * ey * nz,
            (0.5 * r5) * (3.0 * ez * nz - env), r15 * ex * nz, (0.5 * r15) * (ex * nx - ey * ny),
        ]
        for m in range(9):
            ang_s[m] = angular[m]
        for j in range(8):
            rad_s[:, j, :] = jnp.exp(distance * (-1.0 / 2.0**j))
        gathered = []
        for t in range(128):
            acc = None
            for j in range(8):
                v = tab_ref[pl.ds(idx_ref[g * 1024 + (t * 8 + j)] + (table_pad - j), 8), :]
                acc = v if acc is None else jnp.where(sub == j, v, acc)
            gathered.append(acc)
        dst = jnp.concatenate(gathered, axis=0)
        pieces = []
        for r in range(8):
            rad = rad_s[r]
            rad_hi = rad.astype(bf16).astype(f32)
            pieces.append(jnp.concatenate([rad_hi, rad - rad_hi, rad_hi, jnp.zeros_like(rad)], axis=0).astype(bf16))
        rad_ext = jnp.concatenate(pieces, axis=1)
        term = lax.dot_general(rad_ext, w_ext, (((0,), (0,)), ((), ())), preferred_element_type=f32)
        src = src_ref[pl.ds(pl.multiple_of(g * 64, 64), 64), :]
        src = jnp.broadcast_to(src[:, None, :], (64, 16, 128)).reshape(1024, 128)
        half = dst + src + term
        latent = (half + half * jnp.tanh(half)).astype(bf16)
        half = jnp.dot(latent, w_mid, preferred_element_type=f32)
        hidden = half + half * jnp.tanh(half)
        hid_hi = hidden.astype(bf16)
        hid_lo = (hidden - hid_hi.astype(f32)).astype(bf16)
        hid = jnp.concatenate([hid_hi, hid_lo], axis=1)
        zero = jnp.zeros((8, 128), f32)
        for p in range(4):
            blocks_hi, blocks_lo = [], []
            for m in range(9):
                cols_hi, cols_lo = [], []
                for q in range(2):
                    row = jnp.where(diag, jnp.broadcast_to(ang_s[m, 2 * p + q : 2 * p + q + 1, :], (8, 128)), 0.0)
                    row_hi = row.astype(bf16).astype(f32)
                    row_lo = row - row_hi
                    cols_hi.append(jnp.concatenate([row_hi, zero] if q == 0 else [zero, row_hi], axis=0).astype(bf16))
                    cols_lo.append(jnp.concatenate([row_lo, zero] if q == 0 else [zero, row_lo], axis=0).astype(bf16))
                blocks_hi.append(jnp.concatenate(cols_hi, axis=1))
                blocks_lo.append(jnp.concatenate(cols_lo, axis=1))
            both = jnp.concatenate(blocks_hi + blocks_lo, axis=0)
            mom2 = jnp.dot(both, hid[p * 256 : p * 256 + 256], preferred_element_type=f32)
            mom = mom2[:144, :128] + mom2[:144, 128:] + mom2[144:, :128]
            sq = [mom[m * 16 : m * 16 + 16] ** 2 for m in range(9)]
            rr = slice(p * 16, p * 16 + 16)
            inv_s[rr, 0:128] = sq[0]
            inv_s[rr, 128:256] = sq[1] + sq[2] + sq[3]
            inv_s[rr, 256:384] = (sq[4] + sq[5]) + (sq[6] + sq[7]) + sq[8]
        update = jnp.dot(inv_s[...].astype(bf16), wout_ref[...], preferred_element_type=f32)
        arows = pl.ds(pl.multiple_of(g * 64, 64), 64)
        orows = pl.ds(pl.multiple_of(i * 64, 64), 64)
        out_ref[orows, :] = (own_ref[arows, :].astype(f32) + update).astype(bf16)
        return carry

    lax.fori_loop(0, blocks, body, 0)


def edge_call(start, blocks, idx, nb, geo, cnt, tab, src, own, w_rad, w_mid, w_out, after):
    return kernel_call(
        functools.partial(edge_kernel, start=start, blocks=blocks),
        jax.ShapeDtypeStruct((blocks * 64, 128), jnp.bfloat16),
        [SMEM] + [VMEM] * 9 + [ANY],
        [
            pltpu.VMEM((9, 8, 128), jnp.float32),
            pltpu.VMEM((8, 8, 128), jnp.float32),
            pltpu.VMEM((64, 384), jnp.float32),
        ],
        "edges",
        flops=blocks * 2 * 10**9,
        moved=blocks * 6 * 10**6,
    )(idx, nb, geo, cnt, tab, src, own, w_rad, w_mid, w_out, after)


def swap(x, axis):
    return lax.all_to_all(x, axis, split_axis=0, concat_axis=0, tiled=True)


def shifted(x, axis, step):
    size = lax.axis_size(axis)
    return lax.ppermute(x, axis, [(i, (i + step) % size) for i in range(size)])


def local(features, offsets, frac, neighbors, counts, w_src, w_dst, w_rad, w_mid, w_out, w_charge):
    f32, bf16 = jnp.float32, jnp.bfloat16
    own = features[0, 0]
    dom, sub = lax.axis_index("dom"), lax.axis_index("sub")
    anchor = jnp.stack([dom * 4, sub * 64, jnp.zeros_like(dom)]).astype(jnp.int32)
    cells = offsets[:, 0, 0] - anchor[:, None]
    fracs = frac[:, 0, 0]
    place = cells.astype(f32) + fracs
    place_rows = place.reshape(48, 128)

    head = place[:, :head_rows].reshape(12, 128)
    top = lax.reduce_precision(head, 8, 7)
    mid = lax.reduce_precision(head - top, 8, 7)
    low = lax.reduce_precision(head - top - mid, 8, 7)
    sent = jnp.concatenate(
        [own[:head_rows]] + [part.astype(bf16) for part in (top, mid, low)] + [jnp.zeros((12, 128), bf16)], axis=0
    )
    before = shifted(sent, "dom", 1)
    after = shifted(sent, "dom", -1)
    column = jnp.stack([before, sent, after])
    left = shifted(column, "sub", 1)
    right = shifted(column, "sub", -1)

    square, factor = jnp.asarray(wave_square), jnp.asarray(wave_factor)
    pick = lambda table: (table.reshape(4, 64)[:, dom][:, None], table.reshape(4, 64)[sub][None, :])
    square_y, square_z = pick(square)
    factor_y, factor_z = pick(factor)
    row = jnp.stack([(square_y + square_z).reshape(GRID), (factor_y * factor_z).reshape(GRID)])
    col = jnp.stack([square, factor])[:, :, None]

    grid_shape = jax.ShapeDtypeStruct((4, rows_y, 512), f32)
    pencil_shape = jax.ShapeDtypeStruct((64, 1, 2048), f32)
    ext_grid = pltpu.VMEM((ext_x * rows_y, GRID), f32)
    stage = functools.partial(kernel_call, flops=10**9, moved=10**6)

    waves_z = stage(
        spread_kernel, grid_shape, [VMEM] * 6, [ext_grid, pltpu.VMEM((8, 2048), f32)], "spread"
    )(cells, fracs, own, w_charge[None, :], *forward_z)
    tab, src, geo = stage(
        tables_kernel,
        (
            jax.ShapeDtypeStruct((6144 + 2 * table_pad, 128), f32),
            jax.ShapeDtypeStruct((2048, 128), f32),
            jax.ShapeDtypeStruct((144, 128), f32),
        ),
        [VMEM] * 7,
        (),
        "tables",
    )(own, jnp.stack([before, after]), left, right, place_rows, w_src, w_dst)
    pairs = neighbors[0, 0]
    idx, nb = pairs.reshape(-1), pairs.reshape(256, 128)
    live = counts[0, 0].reshape(16, 128)
    edges = lambda start, blocks, later: edge_call(
        start, blocks, idx, nb, geo, live, tab, src, own, w_rad, w_mid, w_out, later
    )
    done_a = edges(0, 8, waves_z)
    waves_y = stage(forward_y_kernel, pencil_shape, [VMEM] * 3 + [ANY], (), "forward_y")(
        swap(waves_z, "sub"), *forward_y, done_a
    )
    done_b = edges(8, 8, waves_y)
    filtered = stage(filter_kernel, pencil_shape, [VMEM] * 7 + [ANY], (), "filter")(
        swap(waves_y, "dom"), *forward_x, *inverse_x, col, row, done_b
    )
    done_c = edges(16, 8, filtered)
    cells_y = stage(inverse_y_kernel, grid_shape, [VMEM] * 3 + [ANY], (), "inverse_y")(
        swap(filtered, "dom"), *inverse_y, done_c
    )
    done_d = edges(24, 8, cells_y)
    potential = stage(
        read_kernel, jax.ShapeDtypeStruct((1, 2048), f32), [VMEM] * 5 + [ANY], [ext_grid], "read"
    )(swap(cells_y, "sub"), cells, fracs, *inverse_z, done_d)
    new_rows = jnp.concatenate([done_a, done_b, done_c, done_d], axis=0)
    return new_rows.reshape(features.shape), potential.reshape(1, 1, 2048)


def solution(mesh):
    placed = (
        P("dom", "sub", None, None),
        P(None, "dom", "sub", None),
        P(None, "dom", "sub", None),
        P("dom", "sub", None, None),
        P("dom", "sub", None),
        P(),
        P(),
        P(),
        P(),
        P(),
        P(),
    )
    return jax.shard_map(
        local,
        mesh=mesh,
        in_specs=placed,
        out_specs=(P("dom", "sub", None, None), P("dom", "sub", None)),
        check_vma=False,
    )
```

time: 910 us -> 162 us (0.18); the launches traced: 896 us -> 161 us
  local copies, waits for them, and re-layouts: 425 us -> 17.9 us
  matrix products: 279 us -> 0 us
  Pallas kernels: 0 us -> 79.7 us
  other arithmetic: 57 us -> 2.04 us
  loops' own time: 33.4 us -> 0 us
  waiting for transfers between devices: 40.9 us -> 14.5 us
  starting transfers between devices: 58.7 us -> 45.8 us
    gather x48 -> x0, local copies, waits for them, and re-layouts: 299 us -> none  [the longest x32 178 us: one_block(): part_geom = geo_table[:, partner]]
    dot_general x83 -> x0, matrix products: 257 us -> none  [the longest x16 66.2 us: edge_update(): radial_term = jnp.einsum('akn,nc->akc', radial, w_rad, precision=highest)]
    pallas_call x0 -> x10, Pallas kernels: none -> 79.7 us  [the longest x4 64.9 us: edge_call(): kernel_call(functools.partial(edge_kernel, start=start, blocks=blocks), j...]
    dynamic_slice x64 -> x1, local copies, waits for them, and re-layouts: 47.8 us -> 0.22 us  [local(): table.reshape(4, 64)[:, dom][:, None]]
    another operation x1 -> x0, loops' own time: 33.4 us -> none  [local(): new_rows = lax.map(one_block, start_rows).reshape(atom_count, channels)]
    all_to_all x4, waiting for transfers between devices: 28.2 us -> 0.01 us  [swap(): return lax.all_to_all(x, axis, split_axis=0, concat_axis=0, tiled=True)]
    select_n x36 -> x0, other arithmetic: 28.2 us -> none  [the longest x16 14.4 us: one_block(): part_geom = geo_table[:, partner]]
    another operation x22 -> x2, local copies, waits for them, and re-layouts: 27.4 us -> 0.61 us  [local(): idx, nb = (pairs.reshape(-1), pairs.reshape(256, 128))]
  transfers between devices with their start and end apart: 16 -> 8, of which waited for: 7 -> 2; matrix products, arithmetic and copies ran while one was open for 81% -> 2% of each run, Pallas kernels for 0% -> 44%
where the time goes in v1:
time: 162 us; the launch traced here: 161 us
  Pallas kernels  79.7 us (49%)
  starting transfers between devices  45.8 us (28%)
  local copies, waits for them, and re-layouts  17.9 us (11%)
  waiting for transfers between devices  14.5 us (9%)
  other arithmetic  2.04 us (1%)
    pallas_call x4, Pallas kernels, edge_call(): kernel_call(functools.partial(edge_kernel, start=start, blocks=blocks), j...  64.9 us
    all_to_all x4, starting transfers between devices, swap(): return lax.all_to_all(x, axis, split_axis=0, concat_axis=0, tiled=True)  32.5 us
    unnamed x72, local copies, waits for them, and re-layouts  15.5 us
    ppermute x4, waiting for transfers between devices, shifted(): return lax.ppermute(x, axis, [(i, (i + step) % size) for i in range(size)])  14.4 us
    ppermute x4, starting transfers between devices, shifted(): return lax.ppermute(x, axis, [(i, (i + step) % size) for i in range(size)])  13.3 us
    pallas_call x1, Pallas kernels, local(): stage(spread_kernel, grid_shape, [VMEM] * 6, [ext_grid, pltpu.VMEM((8, 20...  4.96 us
    pallas_call x1, Pallas kernels, local(): stage(read_kernel, jax.ShapeDtypeStruct((1, 2048), f32), [VMEM] * 5 + [AN...  4.2 us
  transfers between devices with their start and end apart: 8, of which 2 were waited for; matrix products, arithmetic and copies ran while one was open for 2% of the time, Pallas kernels for 44%

profile of v1, /device:TPU:1, one launch (start us, length us, event | category | flops | bytes accessed | tf_op | source)
XLA Modules:
  0.0 160.8 jit_solution(17587126575485762001)
XLA Ops:
  0.6 0.9 slice_bitcast_fusion
  1.6 0.8 copy.34
  2.4 0.8 bitcast_subtract_fusion.cell_ref
  3.6 11.6 %collective-permute-start.1 = (bf16[560,128]{1,0:T(8,128)(2,1)S(1)}, bf16[560,128]{1,0:T(8,128)(2,1)S(1)}, u32[]{:S(2)}, u32[]{:S(2)}) collective-permute-start(bf16[560,128]{1,0:T(8,128)(2,1)S(1)} %concatenate.6), channel_id=1, source_target_pairs={{0,252},{4,0},{8,4},{12,8},{16,12},{20,16},{24,20},{28,24},{32,28}... | collective-permute-start | bytes 430088 | tf_op jit(solution)/shard_map/ppermute | solution.py:374
  15.2 1.0 copy-done
  16.9 0.9 copy-done.20
  17.8 0.9 copy-done.21
  18.7 5.0 %spread.1.after_ref = f32[4,72,512]{2,1,0:T(8,128)} custom-call(s32[3,2048]{1,0:T(4,128)S(1)} %bitcast_subtract_fusion.cell_ref, f32[3,2048]{1,0:T(4,128)S(1)} %bitcast.29, bf16[2048,128]{1,0:T(8,128)(2,1)S(1)} %bitcast.31, f32[1,128]{1,0:T(1,128)S(1)} %bitcast.41, bf16[256,256]{1,0:T(8,128)(2,1)S(1)} %copy-done.20, bf16[256,256]{1,0:T(8,128)(2,1)S(1)} %copy-done.21), custom_call_target="tpu_custom_call" | custom-call | flops 1000000000 | bytes 1000000 | tf_op jit(solution)/shard_map/spread/pallas_call | solution.py:412
  23.7 4.5 %all-to-all-start = ((f32[4,72,512]{2,1,0:T(8,128)}), f32[4,72,512]{2,1,0:T(8,128)S(1)}, u32[]{:S(2)}, u32[]{:S(2)}) async-start(f32[4,72,512]{2,1,0:T(8,128)} %spread.1.after_ref), calls=%async_computation | async-start | bytes 1179648 | tf_op jit(solution)/shard_map/all_to_all | solution.py:369
  30.0 1.7 %collective-permute-start.2 = (bf16[3,560,128]{2,1,0:T(8,128)(2,1)S(1)}, bf16[3,560,128]{2,1,0:T(8,128)(2,1)S(1)}, u32[]{:S(2)}, u32[]{:S(2)}) collective-permute-start(bf16[3,560,128]{2,1,0:T(8,128)(2,1)S(1)} %pad_maximum_fusion), channel_id=1, source_target_pairs={{0,1},{1,2},{2,3},{3,0},{4,5},{5,6},{6,7},{7,4},{8,9},{9,10},{10,1... | collective-permute-start | bytes 1290248 | tf_op jit(solution)/shard_map/ppermute | solution.py:374
  31.8 12.4 %collective-permute-done.2.left_ref = bf16[3,560,128]{2,1,0:T(8,128)(2,1)S(1)} collective-permute-done((bf16[3,560,128]{2,1,0:T(8,128)(2,1)S(1)}, bf16[3,560,128]{2,1,0:T(8,128)(2,1)S(1)}, u32[]{:S(2)}, u32[]{:S(2)}) %collective-permute-start.2) | collective-permute-done | bytes 430112 | tf_op jit(solution)/shard_map/ppermute | solution.py:374
  44.2 2.0 %collective-permute-done.3.right_ref = bf16[3,560,128]{2,1,0:T(8,128)(2,1)S(1)} collective-permute-done((bf16[3,560,128]{2,1,0:T(8,128)(2,1)S(1)}, bf16[3,560,128]{2,1,0:T(8,128)(2,1)S(1)}, u32[]{:S(2)}, u32[]{:S(2)}) %collective-permute-start.3) | collective-permute-done | bytes 430112 | tf_op jit(solution)/shard_map/ppermute | solution.py:374
  46.3 0.7 tables.1
  47.1 16.3 %edges.4.after_ref = bf16[512,128]{1,0:T(8,128)(2,1)S(1)} custom-call(s32[32768]{0:T(1024)S(1)} %reshape_squeeze.9.idx_ref, s32[256,128]{1,0:T(8,128)S(1)} %reshape_squeeze.10.nb_ref, f32[144,128]{1,0:T(8,128)S(1)} %get-tuple-element.5.geo_ref, s32[16,128]{1,0:T(8,128)S(1)} %bitcast.37, f32[6160,128]{1,0:T(8,128)S(1)} %get-tuple-element.6.tab_ref, ...), custom_call_target="tpu_custom_call" | custom-call | flops 16000000000 | bytes 48000000 | tf_op jit(solution)/shard_map/edges/pallas_call | solution.py:353
  63.3 1.7 %copy-done.22 = f32[6160,128]{1,0:T(8,128)} copy-done((f32[6160,128]{1,0:T(8,128)}, f32[6160,128]{1,0:T(8,128)S(1)}, u32[]{:S(2)}) %copy-start.22) | copy-done | bytes 3153944
  65.0 1.0 copy-done.26
  66.0 1.4 forward_y.1.after_ref
  67.4 10.5 %all-to-all-start.1 = ((f32[64,1,2048]{2,1,0:T(1,128)}), f32[64,1,2048]{2,1,0:T(1,128)S(1)}, u32[]{:S(2)}, u32[]{:S(2)}) async-start(f32[64,1,2048]{2,1,0:T(1,128)} %forward_y.1.after_ref), calls=%async_computation.1 | async-start | bytes 1048576 | tf_op jit(solution)/shard_map/all_to_all | solution.py:369
  77.9 1.9 %copy-done.23 = f32[6160,128]{1,0:T(8,128)S(1)} copy-done((f32[6160,128]{1,0:T(8,128)S(1)}, f32[6160,128]{1,0:T(8,128)}, u32[]{:S(2)}) %copy-start.23) | copy-done | bytes 3153944
  79.8 1.2 copy-done.27
  81.1 16.2 %edges.5.after_ref = bf16[512,128]{1,0:T(8,128)(2,1)S(1)} custom-call(s32[32768]{0:T(1024)S(1)} %reshape_squeeze.9.idx_ref, s32[256,128]{1,0:T(8,128)S(1)} %reshape_squeeze.10.nb_ref, f32[144,128]{1,0:T(8,128)S(1)} %get-tuple-element.5.geo_ref, s32[16,128]{1,0:T(8,128)S(1)} %bitcast.38, f32[6160,128]{1,0:T(8,128)S(1)} %copy-done.23, ...), custom_call_target="tpu_custom_call" | custom-call | flops 16000000000 | bytes 48000000 | tf_op jit(solution)/shard_map/edges/pallas_call | solution.py:353
  97.3 2.2 %filter.1.after_ref = f32[64,1,2048]{2,1,0:T(1,128)} custom-call(f32[64,1,2048]{2,1,0:T(1,128)S(1)} %all-to-all-done.1.x_ref, bf16[256,448]{1,0:T(8,128)(2,1)S(1)} %copy-done.9, bf16[256,448]{1,0:T(8,128)(2,1)S(1)} %copy-done.10, bf16[448,256]{1,0:T(8,128)(2,1)S(1)} %copy-done.12, bf16[448,256]{1,0:T(8,128)(2,1)S(1)} %copy-done.13, ...), custom_call_target="tpu_custom_call" | custom-call | flops 1000000000 | bytes 1000000 | tf_op jit(solution)/shard_map/filter/pallas_call | solution.py:437
  99.5 12.0 %all-to-all-start.2 = ((f32[64,1,2048]{2,1,0:T(1,128)}), f32[64,1,2048]{2,1,0:T(1,128)S(1)}, u32[]{:S(2)}, u32[]{:S(2)}) async-start(f32[64,1,2048]{2,1,0:T(1,128)} %filter.1.after_ref), calls=%async_computation.2 | async-start | bytes 1048576 | tf_op jit(solution)/shard_map/all_to_all | solution.py:369
  111.6 1.9 %copy-done.24 = f32[6160,128]{1,0:T(8,128)S(1)} copy-done((f32[6160,128]{1,0:T(8,128)S(1)}, f32[6160,128]{1,0:T(8,128)}, u32[]{:S(2)}) %copy-start.24) | copy-done | bytes 3153944
  113.5 1.2 copy-done.28
  114.7 16.2 %edges.6.after_ref = bf16[512,128]{1,0:T(8,128)(2,1)S(1)} custom-call(s32[32768]{0:T(1024)S(1)} %reshape_squeeze.9.idx_ref, s32[256,128]{1,0:T(8,128)S(1)} %reshape_squeeze.10.nb_ref, f32[144,128]{1,0:T(8,128)S(1)} %get-tuple-element.5.geo_ref, s32[16,128]{1,0:T(8,128)S(1)} %bitcast.39, f32[6160,128]{1,0:T(8,128)S(1)} %copy-done.24, ...), custom_call_target="tpu_custom_call" | custom-call | flops 16000000000 | bytes 48000000 | tf_op jit(solution)/shard_map/edges/pallas_call | solution.py:353
  130.9 1.3 inverse_y.1.after_ref
  132.2 5.5 %all-to-all-start.3 = ((f32[4,72,512]{2,1,0:T(8,128)}), f32[4,72,512]{2,1,0:T(8,128)S(1)}, u32[]{:S(2)}, u32[]{:S(2)}) async-start(f32[4,72,512]{2,1,0:T(8,128)} %inverse_y.1.after_ref), calls=%async_computation.3 | async-start | bytes 1179648 | tf_op jit(solution)/shard_map/all_to_all | solution.py:369
  137.7 1.9 %copy-done.25 = f32[6160,128]{1,0:T(8,128)S(1)} copy-done((f32[6160,128]{1,0:T(8,128)S(1)}, f32[6160,128]{1,0:T(8,128)}, u32[]{:S(2)}) %copy-start.25) | copy-done | bytes 3153944
  139.6 16.2 %edges.7.after_ref = bf16[512,128]{1,0:T(8,128)(2,1)S(1)} custom-call(s32[32768]{0:T(1024)S(1)} %reshape_squeeze.9.idx_ref, s32[256,128]{1,0:T(8,128)S(1)} %reshape_squeeze.10.nb_ref, f32[144,128]{1,0:T(8,128)S(1)} %get-tuple-element.5.geo_ref, s32[16,128]{1,0:T(8,128)S(1)} %bitcast.40, f32[6160,128]{1,0:T(8,128)S(1)} %copy-done.25, ...), custom_call_target="tpu_custom_call" | custom-call | flops 16000000000 | bytes 48000000 | tf_op jit(solution)/shard_map/edges/pallas_call | solution.py:353
  155.8 0.8 maximum_bitcast_fusion
  156.6 4.2 %read.1 = f32[1,2048]{1,0:T(1,128)} custom-call(f32[4,72,512]{2,1,0:T(8,128)S(1)} %all-to-all-done.3.x_ref, s32[3,2048]{1,0:T(4,128)S(1)} %bitcast_subtract_fusion.cell_ref, f32[3,2048]{1,0:T(4,128)S(1)} %bitcast.30, bf16[256,256]{1,0:T(8,128)(2,1)S(1)} %copy-done.18, bf16[256,256]{1,0:T(8,128)(2,1)S(1)} %copy-done.19, bf16[512,128]{1,0:T(8,128)(2,1)S(1)} %edges.7.after_ref), custom_call_target="tpu_custom_call" | custom-call | flops 1000000000 | bytes 1000000 | tf_op jit(solution)/shard_map/read/pallas_call | solution.py:445
  (89 shorter events, 3.0 us)
Async XLA Ops:
  0.6 27.6 %copy-start.30 = (s32[1,1,2048,16]{2,3,1,0:T(8,128)S(1)}, s32[1,1,2048,16]{2,3,1,0:T(8,128)}, u32[]{:S(2)}) copy-start(s32[1,1,2048,16]{2,3,1,0:T(8,128)} %param.28) | copy-start | bytes 393220
  3.6 26.3 %collective-permute-start.1 = (bf16[560,128]{1,0:T(8,128)(2,1)S(1)}, bf16[560,128]{1,0:T(8,128)(2,1)S(1)}, u32[]{:S(2)}, u32[]{:S(2)}) collective-permute-start(bf16[560,128]{1,0:T(8,128)(2,1)S(1)} %concatenate.6), channel_id=1, source_target_pairs={{0,252},{4,0},{8,4},{12,8},{16,12},{20,16},{24,20},{28,24},{32,28}... | collective-permute-start | bytes 430088 | tf_op jit(solution)/shard_map/ppermute | solution.py:374
  15.2 14.8 %collective-permute-start = (bf16[560,128]{1,0:T(8,128)(2,1)S(1)}, bf16[560,128]{1,0:T(8,128)(2,1)S(1)}, u32[]{:S(2)}, u32[]{:S(2)}) collective-permute-start(bf16[560,128]{1,0:T(8,128)(2,1)S(1)} %concatenate.6), channel_id=1, source_target_pairs={{0,4},{4,8},{8,12},{12,16},{16,20},{20,24},{24,28},{28,32},{32,36}... | collective-permute-start | bytes 430088 | tf_op jit(solution)/shard_map/ppermute | solution.py:374
  23.6 5.7 %copy-start.33 = (f32[4,64]{1,0:T(4,128)S(1)}, f32[4,64]{1,0:T(4,128)}, u32[]{:S(2)}) copy-start(f32[4,64]{1,0:T(4,128)} %constant.70) | copy-start | bytes 3076
  23.6 5.7 %copy-start.34 = (f32[4,64]{1,0:T(4,128)S(1)}, f32[4,64]{1,0:T(4,128)}, u32[]{:S(2)}) copy-start(f32[4,64]{1,0:T(4,128)} %constant.71) | copy-start | bytes 3076
  23.6 8.1 %copy-start.31 = (f32[3,1,1,2048]{3,2,1,0:T(1,128)S(1)}, f32[3,1,1,2048]{3,2,1,0:T(1,128)}, u32[]{:S(2)}) copy-start(f32[3,1,1,2048]{3,2,1,0:T(1,128)} %param.27) | copy-start | bytes 73732
  23.6 8.1 %copy-start.32 = (s32[3,1,1,2048]{3,2,1,0:T(1,128)S(1)}, s32[3,1,1,2048]{3,2,1,0:T(1,128)}, u32[]{:S(2)}) copy-start(s32[3,1,1,2048]{3,2,1,0:T(1,128)} %param.26) | copy-start | bytes 73732
  23.6 22.6 %copy-start.1 = (bf16[1,1,2048,128]{3,2,1,0:T(8,128)(2,1)S(1)}, bf16[1,1,2048,128]{3,2,1,0:T(8,128)(2,1)}, u32[]{:S(2)}) copy-start(bf16[1,1,2048,128]{3,2,1,0:T(8,128)(2,1)} %param.25) | copy-start | bytes 1572868
  23.7 22.6 %copy-start.3 = (bf16[128,128]{1,0:T(8,128)(2,1)S(1)}, bf16[128,128]{1,0:T(8,128)(2,1)}, u32[]{:S(2)}) copy-start(bf16[128,128]{1,0:T(8,128)(2,1)} %wsrc_ref.1) | copy-start | bytes 98308
  23.7 22.6 %copy-start.4 = (bf16[128,128]{1,0:T(8,128)(2,1)S(1)}, bf16[128,128]{1,0:T(8,128)(2,1)}, u32[]{:S(2)}) copy-start(bf16[128,128]{1,0:T(8,128)(2,1)} %wdst_ref.1) | copy-start | bytes 98308
  23.7 42.3 %all-to-all-start = ((f32[4,72,512]{2,1,0:T(8,128)}), f32[4,72,512]{2,1,0:T(8,128)S(1)}, u32[]{:S(2)}, u32[]{:S(2)}) async-start(f32[4,72,512]{2,1,0:T(8,128)} %spread.1.after_ref), calls=%async_computation | async-start | bytes 1179648 | tf_op jit(solution)/shard_map/all_to_all | solution.py:369
  28.9 18.1 %copy-start.2 = (bf16[384,128]{1,0:T(8,128)(2,1)S(1)}, bf16[384,128]{1,0:T(8,128)(2,1)}, u32[]{:S(2)}) copy-start(bf16[384,128]{1,0:T(8,128)(2,1)} %wout_ref.7) | copy-start | bytes 294916
  28.9 18.1 %copy-start.5 = (bf16[128,128]{1,0:T(8,128)(2,1)S(1)}, bf16[128,128]{1,0:T(8,128)(2,1)}, u32[]{:S(2)}) copy-start(bf16[128,128]{1,0:T(8,128)(2,1)} %wmid_ref.7) | copy-start | bytes 98308
  28.9 18.1 %copy-start.6 = (s32[1,1,2048]{2,1,0:T(1,128)S(1)}, s32[1,1,2048]{2,1,0:T(1,128)}, u32[]{:S(2)}) copy-start(s32[1,1,2048]{2,1,0:T(1,128)} %param.29) | copy-start | bytes 24580
  28.9 18.1 %copy-start.7 = (f32[8,128]{1,0:T(8,128)S(1)}, f32[8,128]{1,0:T(8,128)}, u32[]{:S(2)}) copy-start(f32[8,128]{1,0:T(8,128)} %wrad_ref.7) | copy-start | bytes 12292
  30.0 14.3 %collective-permute-start.2 = (bf16[3,560,128]{2,1,0:T(8,128)(2,1)S(1)}, bf16[3,560,128]{2,1,0:T(8,128)(2,1)S(1)}, u32[]{:S(2)}, u32[]{:S(2)}) collective-permute-start(bf16[3,560,128]{2,1,0:T(8,128)(2,1)S(1)} %pad_maximum_fusion), channel_id=1, source_target_pairs={{0,1},{1,2},{2,3},{3,0},{4,5},{5,6},{6,7},{7,4},{8,9},{9,10},{10,1... | collective-permute-start | bytes 1290248 | tf_op jit(solution)/shard_map/ppermute | solution.py:374
  31.7 14.6 %collective-permute-start.3 = (bf16[3,560,128]{2,1,0:T(8,128)(2,1)S(1)}, bf16[3,560,128]{2,1,0:T(8,128)(2,1)S(1)}, u32[]{:S(2)}, u32[]{:S(2)}) collective-permute-start(bf16[3,560,128]{2,1,0:T(8,128)(2,1)S(1)} %pad_maximum_fusion), channel_id=1, source_target_pairs={{0,3},{1,0},{2,1},{3,2},{4,7},{5,4},{6,5},{7,6},{8,11},{9,8},{10,9... | collective-permute-start | bytes 1290248 | tf_op jit(solution)/shard_map/ppermute | solution.py:374
  47.0 18.9 %copy-start.14 = (bf16[256,288]{1,0:T(8,128)(2,1)S(1)}, bf16[256,288]{1,0:T(8,128)(2,1)}, u32[]{:S(2)}) copy-start(bf16[256,288]{1,0:T(8,128)(2,1)} %constant.51.clone.thi_ref) | copy-start | bytes 442372
  47.0 18.9 %copy-start.15 = (bf16[256,288]{1,0:T(8,128)(2,1)S(1)}, bf16[256,288]{1,0:T(8,128)(2,1)}, u32[]{:S(2)}) copy-start(bf16[256,288]{1,0:T(8,128)(2,1)} %constant.52.clone.tlo_ref) | copy-start | bytes 442372
  67.4 29.9 %all-to-all-start.1 = ((f32[64,1,2048]{2,1,0:T(1,128)}), f32[64,1,2048]{2,1,0:T(1,128)S(1)}, u32[]{:S(2)}, u32[]{:S(2)}) async-start(f32[64,1,2048]{2,1,0:T(1,128)} %forward_y.1.after_ref), calls=%async_computation.1 | async-start | bytes 1048576 | tf_op jit(solution)/shard_map/all_to_all | solution.py:369
  81.0 16.3 %copy-start.9 = (bf16[256,448]{1,0:T(8,128)(2,1)S(1)}, bf16[256,448]{1,0:T(8,128)(2,1)}, u32[]{:S(2)}) copy-start(bf16[256,448]{1,0:T(8,128)(2,1)} %constant.53.clone.thi_ref) | copy-start | bytes 688132
  81.0 16.3 %copy-start.10 = (bf16[256,448]{1,0:T(8,128)(2,1)S(1)}, bf16[256,448]{1,0:T(8,128)(2,1)}, u32[]{:S(2)}) copy-start(bf16[256,448]{1,0:T(8,128)(2,1)} %constant.54.clone.tlo_ref) | copy-start | bytes 688132
  81.0 16.3 %copy-start.11 = (f32[2,256,1]{2,1,0:T(8,128)S(1)}, f32[2,256,1]{2,1,0:T(8,128)}, u32[]{:S(2)}) copy-start(f32[2,256,1]{2,1,0:T(8,128)} %constant.69.col_ref) | copy-start | bytes 6148
  81.0 16.3 %copy-start.12 = (bf16[448,256]{1,0:T(8,128)(2,1)S(1)}, bf16[448,256]{1,0:T(8,128)(2,1)}, u32[]{:S(2)}) copy-start(bf16[448,256]{1,0:T(8,128)(2,1)} %constant.55.clone.uhi_ref) | copy-start | bytes 688132
  81.1 16.3 %copy-start.13 = (bf16[448,256]{1,0:T(8,128)(2,1)S(1)}, bf16[448,256]{1,0:T(8,128)(2,1)}, u32[]{:S(2)}) copy-start(bf16[448,256]{1,0:T(8,128)(2,1)} %constant.56.clone.ulo_ref) | copy-start | bytes 688132
  99.5 31.4 %all-to-all-start.2 = ((f32[64,1,2048]{2,1,0:T(1,128)}), f32[64,1,2048]{2,1,0:T(1,128)S(1)}, u32[]{:S(2)}, u32[]{:S(2)}) async-start(f32[64,1,2048]{2,1,0:T(1,128)} %filter.1.after_ref), calls=%async_computation.2 | async-start | bytes 1048576 | tf_op jit(solution)/shard_map/all_to_all | solution.py:369
  114.7 16.2 %copy-start.16 = (bf16[288,256]{1,0:T(8,128)(2,1)S(1)}, bf16[288,256]{1,0:T(8,128)(2,1)}, u32[]{:S(2)}) copy-start(bf16[288,256]{1,0:T(8,128)(2,1)} %constant.57.clone.thi_ref) | copy-start | bytes 442372
  114.7 16.2 %copy-start.17 = (bf16[288,256]{1,0:T(8,128)(2,1)S(1)}, bf16[288,256]{1,0:T(8,128)(2,1)}, u32[]{:S(2)}) copy-start(bf16[288,256]{1,0:T(8,128)(2,1)} %constant.58.clone.tlo_ref) | copy-start | bytes 442372
  130.9 6.8 %copy-start.29 = (f32[2048,128]{1,0:T(8,128)S(1)}, f32[2048,128]{1,0:T(8,128)}, u32[]{:S(2)}) copy-start(f32[2048,128]{1,0:T(8,128)} %copy-done.26) | copy-start | bytes 3145732
  132.2 24.4 %all-to-all-start.3 = ((f32[4,72,512]{2,1,0:T(8,128)}), f32[4,72,512]{2,1,0:T(8,128)S(1)}, u32[]{:S(2)}, u32[]{:S(2)}) async-start(f32[4,72,512]{2,1,0:T(8,128)} %inverse_y.1.after_ref), calls=%async_computation.3 | async-start | bytes 1179648 | tf_op jit(solution)/shard_map/all_to_all | solution.py:369
  139.6 17.1 %copy-start.18 = (bf16[256,256]{1,0:T(8,128)(2,1)S(1)}, bf16[256,256]{1,0:T(8,128)(2,1)}, u32[]{:S(2)}) copy-start(bf16[256,256]{1,0:T(8,128)(2,1)} %constant.59.clone.thi_ref) | copy-start | bytes 393220
  139.6 17.1 %copy-start.19 = (bf16[256,256]{1,0:T(8,128)(2,1)S(1)}, bf16[256,256]{1,0:T(8,128)(2,1)}, u32[]{:S(2)}) copy-start(bf16[256,256]{1,0:T(8,128)(2,1)} %constant.60.clone.tlo_ref) | copy-start | bytes 393220
  (11 other events, 14.3 us)

commit v2 on v1

v2 whole, which is shorter than its diff:
```python
import functools
import math

import jax
import jax.numpy as jnp
import ml_dtypes
import numpy as np
from jax import lax
from jax.experimental import pallas as pl
from jax.experimental.pallas import tpu as pltpu
from jax.sharding import PartitionSpec as P

GRID = 256
ext_x = 7
ext_y = 67
rows_y = 72
head_rows = 512
table_pad = 8
edge_split = (10, 21)
halo_places = [(0, 0), (0, 1), (0, 2), (1, 0), (1, 2), (2, 0), (2, 1), (2, 2)]


def split_table(table):
    high = table.astype(ml_dtypes.bfloat16)
    low = (table - high.astype(np.float64)).astype(ml_dtypes.bfloat16)
    return high, low


def real_basis():
    cells = np.arange(GRID)
    basis = np.zeros((GRID, GRID))
    for k in range(GRID):
        wave = k if k <= GRID // 2 else k - GRID // 2
        angle = 2.0 * np.pi / GRID * ((wave * cells) % GRID)
        scale = math.sqrt((1.0 if k in (0, GRID // 2) else 2.0) / GRID)
        basis[k] = scale * (np.cos(angle) if k <= GRID // 2 else np.sin(angle))
    return basis


def wave_tables():
    index = np.arange(GRID)
    wave = np.where(index <= GRID // 2, index, index - GRID // 2) / GRID
    factor = (2.0 + np.cos(2.0 * np.pi * wave)) / 3.0
    return (wave**2).astype(np.float32), (1.0 / factor**2).astype(np.float32)


basis = real_basis()
columns_y = np.zeros((GRID, 4 * rows_y))
for c in range(4):
    for y in range(ext_y):
        columns_y[:, c * rows_y + y] = basis[:, (64 * c - 1 + y) % GRID]
columns_x = np.concatenate([basis[:, (4 * np.arange(64) - 1 + x) % GRID] for x in range(ext_x)], axis=1)
forward_z = split_table(basis.T.copy())
inverse_z = split_table(basis)
forward_y = split_table(columns_y)
inverse_y = split_table(columns_y.T.copy())
forward_x = split_table(columns_x)
inverse_x = split_table(columns_x.T.copy())
wave_square, wave_factor = wave_tables()

def halves(x):
    high = x.astype(jnp.bfloat16)
    return high, (x - high.astype(jnp.float32)).astype(jnp.bfloat16)


def dot_split(a, b, pattern=(((1,), (0,)), ((), ()))):
    dot = functools.partial(lax.dot_general, dimension_numbers=pattern, preferred_element_type=jnp.float32)
    return dot(a[0], b[0]) + (dot(a[0], b[1]) + dot(a[1], b[0]))


def spline_four(f):
    g = 1.0 - f
    f2 = f * f
    f3 = f2 * f
    return (
        g * g * g * (1.0 / 6.0),
        (3.0 * f3 - 6.0 * f2 + 4.0) * (1.0 / 6.0),
        (-3.0 * f3 + 3.0 * f2 + 3.0 * f + 1.0) * (1.0 / 6.0),
        f3 * (1.0 / 6.0),
    )


def placed_weights(count, cell, f, wraps=False):
    ids = lax.broadcasted_iota(jnp.int32, (count, cell.shape[1]), 0)
    step = ids - cell
    if wraps:
        step = (step + 1) & (GRID - 1)
    result = jnp.zeros(step.shape, jnp.float32)
    for k, weight in enumerate(spline_four(f)):
        result = jnp.where(step == k, weight, result)
    return result


def pair_tiles(first, second, half):
    lane = lax.broadcasted_iota(jnp.int32, first.shape, 1)
    if half == 0:
        return jnp.where(lane < 64, first, pltpu.roll(second, 64, 1))
    return jnp.where(lane < 64, pltpu.roll(first, 64, 1), second)


def charge_row(feat_ref, w_ref):
    f32, bf16 = jnp.float32, jnp.bfloat16
    w = jnp.broadcast_to(w_ref[...], (16, 128))
    top = w.astype(bf16).astype(f32)
    mid = (w - top).astype(bf16).astype(f32)
    sub = lax.broadcasted_iota(jnp.int32, (16, 128), 0)
    parts = jnp.where(sub == 0, top, jnp.where(sub == 1, mid, jnp.where(sub == 2, w - top - mid, 0.0))).astype(bf16)
    raw = lax.dot_general(parts, feat_ref[...], (((1,), (1,)), ((), ())), preferred_element_type=f32)
    raw = jnp.broadcast_to(raw[0:1] + raw[1:2] + raw[2:3], (8, raw.shape[1]))
    lane = lax.broadcasted_iota(jnp.int32, raw.shape, 1)
    mate = jnp.where(lane % 2 == 0, pltpu.roll(raw, raw.shape[1] - 1, 1), pltpu.roll(raw, 1, 1))
    return 0.5 * (raw - mate)


def spread(cell_ref, frac_ref, charge_s, along_s, grid_s, table, out_ref):
    grid_s[...] = jnp.zeros_like(grid_s)

    def tile(i, carry):
        cols = pl.ds(pl.multiple_of(i * 512, 512), 512)
        along_x = placed_weights(8, cell_ref[0:1, cols], frac_ref[0:1, cols]) * charge_s[0:1, cols]
        along_y = placed_weights(rows_y, cell_ref[1:2, cols], frac_ref[1:2, cols])
        along_z = halves(placed_weights(GRID, cell_ref[2:3, cols], frac_ref[2:3, cols], True))
        along_s[0, :, cols] = along_z[0]
        along_s[1, :, cols] = along_z[1]
        plane = jnp.concatenate([along_x[x : x + 1] * along_y for x in range(ext_x)], axis=0)
        grid_s[...] += dot_split(halves(plane), along_z, (((1,), (1,)), ((), ())))
        return carry

    lax.fori_loop(0, 4, tile, 0)
    waves = dot_split(halves(grid_s[...]), table)
    for q in range(4):
        for c in range(4):
            cols = slice(128 * (c // 2), 128 * (c // 2) + 128)
            first = waves[2 * q * rows_y : (2 * q + 1) * rows_y, cols]
            if 2 * q + 1 < ext_x:
                second = waves[(2 * q + 1) * rows_y : (2 * q + 2) * rows_y, cols]
            else:
                second = jnp.zeros_like(first)
            out_ref[c, :, q * 128 : q * 128 + 128] = pair_tiles(first, second, c % 2)


def forward_y_step(x_ref, table, out_ref):
    waves = dot_split(table, halves(jnp.concatenate([x_ref[c] for c in range(4)], axis=0)))
    for j in range(4):
        out_ref[:, 0, j * 512 : j * 512 + 512] = waves[64 * j : 64 * j + 64]


def influence_block(col_ref, row_ref):
    square = col_ref[0] + row_ref[0:1, :]
    factor = col_ref[1] * row_ref[1:2, :]
    positive = square > 0.0
    safe = jnp.where(positive, square, 1.0)
    return jnp.where(positive, 16.0 * jnp.exp(square * (-(math.pi**2))) / safe * factor, 0.0)


def filter_step(x_ref, table, back, influence_ref, out_ref):
    slabs = [x_ref[:, 0, j * 512 : j * 512 + 512] for j in range(4)]
    pieces = []
    for x in range(ext_x):
        cols = slice(128 * (x // 2), 128 * (x // 2) + 128)
        pieces.append(
            jnp.concatenate(
                [pair_tiles(slabs[2 * p][:, cols], slabs[2 * p + 1][:, cols], x % 2) for p in range(2)], axis=1
            )
        )
    waves = dot_split(table, halves(jnp.concatenate(pieces, axis=0)))
    cells = dot_split(back, halves(waves * influence_ref[...]))
    for j in range(4):
        for q in range(4):
            cols = slice(128 * (j // 2), 128 * (j // 2) + 128)
            first = cells[128 * q : 128 * q + 64, cols]
            if 2 * q + 1 < ext_x:
                second = cells[128 * q + 64 : 128 * q + 128, cols]
            else:
                second = jnp.zeros_like(first)
            out_ref[:, 0, j * 512 + q * 128 : j * 512 + q * 128 + 128] = pair_tiles(first, second, j % 2)


def inverse_y_step(x_ref, table, out_ref):
    data = jnp.concatenate([x_ref[:, 0, j * 512 : j * 512 + 512] for j in range(4)], axis=0)
    cells = dot_split(table, halves(data))
    for c in range(4):
        out_ref[c] = cells[c * rows_y : (c + 1) * rows_y]


def read_step(x_ref, cell_ref, frac_ref, along_s, table, out_ref, grid_s):
    pieces = []
    for x in range(ext_x):
        cols = slice(128 * (x // 2), 128 * (x // 2) + 128)
        pieces.append(
            jnp.concatenate(
                [pair_tiles(x_ref[2 * p, :, cols], x_ref[2 * p + 1, :, cols], x % 2) for p in range(2)], axis=1
            )
        )
    grid_s[...] = dot_split(halves(jnp.concatenate(pieces, axis=0)), table)

    def tile(i, carry):
        cols = pl.ds(pl.multiple_of(i * 512, 512), 512)
        along_x = placed_weights(8, cell_ref[0:1, cols], frac_ref[0:1, cols])
        along_y = placed_weights(rows_y, cell_ref[1:2, cols], frac_ref[1:2, cols])
        lines = dot_split(halves(grid_s[...]), (along_s[0, :, cols], along_s[1, :, cols]))
        total = jnp.zeros(along_y.shape, jnp.float32)
        for x in range(ext_x):
            total = total + along_x[x : x + 1] * lines[x * rows_y : (x + 1) * rows_y]
        out_ref[:, cols] = jnp.sum(total * along_y, axis=0, keepdims=True)
        return carry

    lax.fori_loop(0, 4, tile, 0)


def geometry_step(g, nb_ref, cnt_ref, geo_s, ang_s, rad_s):
    f32 = jnp.float32
    sub = lax.broadcasted_iota(jnp.int32, (8, 128), 0)
    lane = lax.broadcasted_iota(jnp.int32, (8, 128), 1)
    rows = pl.ds(pl.multiple_of(g * 8, 8), 8)
    nb = nb_ref[rows, :]
    low = nb & 127
    high = nb >> 7
    part = [jnp.zeros((8, 128), f32) for _ in range(3)]
    for h in range(48):
        hit = high == h
        for c in range(3):
            row = jnp.broadcast_to(geo_s[c * 48 + h : c * 48 + h + 1, :], (8, 128))
            part[c] = jnp.where(hit, jnp.take_along_axis(row, low, axis=1), part[c])
    centre = (g % 2) * 64 + sub * 8 + lane // 16
    spot = lambda ref, row: jnp.take_along_axis(jnp.broadcast_to(ref[pl.ds(row, 1), :], (8, 128)), centre, axis=1)
    mine = [spot(geo_s, c * 48 + g // 2) for c in range(3)]
    live = spot(cnt_ref, g // 2)
    dx = part[0] - mine[0]
    dy = part[1] - mine[1]
    dz = part[2] - mine[2]
    cells = jnp.floor(part[2]) - jnp.floor(mine[2])
    dz = jnp.where(cells >= 128.0, dz - 256.0, jnp.where(cells < -128.0, dz + 256.0, dz))
    squared = dx * dx + dy * dy + dz * dz + 1.0
    distance = jnp.sqrt(squared)
    inverse = 1.0 / distance
    nx, ny, nz = dx * inverse, dy * inverse, dz * inverse
    env = jnp.where((lane % 16) < live, 1.0 / (1.0 + squared * (1.0 / 4096.0)), 0.0)
    r3, r5, r15 = math.sqrt(3.0), math.sqrt(5.0), math.sqrt(15.0)
    ex, ey, ez = env * nx, env * ny, env * nz
    angular = [
        env, r3 * ex, r3 * ey, r3 * ez, r15 * ex * ny, r15 * ey * nz,
        (0.5 * r5) * (3.0 * ez * nz - env), r15 * ex * nz, (0.5 * r15) * (ex * nx - ey * ny),
    ]
    for m in range(9):
        ang_s[m, rows, :] = angular[m]
    for j in range(8):
        rad_s[rows, j, :] = jnp.exp(distance * (-1.0 / 2.0**j))


def edge_step(g, w_ext, w_mid, w_out, idx_ref, own_ref, tab_s, src_s, ang_s, rad_s, inv_s, out_ref):
    f32, bf16 = jnp.float32, jnp.bfloat16
    sub = lax.broadcasted_iota(jnp.int32, (8, 128), 0)
    diag = (lax.broadcasted_iota(jnp.int32, (8, 128), 1) // 16) == sub
    gathered = []
    for t in range(128):
        acc = None
        for j in range(8):
            v = tab_s[pl.ds(idx_ref[g * 1024 + (t * 8 + j)] + (table_pad - j), 8), :]
            acc = v if acc is None else jnp.where(sub == j, v, acc)
        gathered.append(acc)
    dst = jnp.concatenate(gathered, axis=0)
    pieces = []
    for r in range(8):
        rad = rad_s[g * 8 + r]
        rad_hi = rad.astype(bf16).astype(f32)
        pieces.append(jnp.concatenate([rad_hi, rad - rad_hi, rad_hi, jnp.zeros_like(rad)], axis=0).astype(bf16))
    rad_ext = jnp.concatenate(pieces, axis=1)
    term = lax.dot_general(rad_ext, w_ext, (((0,), (0,)), ((), ())), preferred_element_type=f32)
    arows = pl.ds(pl.multiple_of(g * 64, 64), 64)
    src = jnp.broadcast_to(src_s[arows, :][:, None, :], (64, 16, 128)).reshape(1024, 128)
    half = dst + src + term
    latent = (half + half * jnp.tanh(half)).astype(bf16)
    half = jnp.dot(latent, w_mid, preferred_element_type=f32)
    hidden = half + half * jnp.tanh(half)
    hid = jnp.concatenate(halves(hidden), axis=1)
    zero = jnp.zeros((8, 128), f32)
    for p in range(4):
        blocks_hi, blocks_lo = [], []
        for m in range(9):
            cols_hi, cols_lo = [], []
            for q in range(2):
                line = ang_s[m, pl.ds(g * 8 + (2 * p + q), 1), :]
                row = jnp.where(diag, jnp.broadcast_to(line, (8, 128)), 0.0)
                row_hi = row.astype(bf16).astype(f32)
                row_lo = row - row_hi
                cols_hi.append(jnp.concatenate([row_hi, zero] if q == 0 else [zero, row_hi], axis=0).astype(bf16))
                cols_lo.append(jnp.concatenate([row_lo, zero] if q == 0 else [zero, row_lo], axis=0).astype(bf16))
            blocks_hi.append(jnp.concatenate(cols_hi, axis=1))
            blocks_lo.append(jnp.concatenate(cols_lo, axis=1))
        both = jnp.concatenate(blocks_hi + blocks_lo, axis=0)
        mom2 = jnp.dot(both, hid[p * 256 : p * 256 + 256], preferred_element_type=f32)
        mom = mom2[:144, :128] + mom2[:144, 128:] + mom2[144:, :128]
        sq = [mom[m * 16 : m * 16 + 16] ** 2 for m in range(9)]
        rows = slice(p * 16, p * 16 + 16)
        inv_s[rows, 0:128] = sq[0]
        inv_s[rows, 128:256] = sq[1] + sq[2] + sq[3]
        inv_s[rows, 256:384] = (sq[4] + sq[5]) + (sq[6] + sq[7]) + sq[8]
    update = jnp.dot(inv_s[...].astype(bf16), w_out, preferred_element_type=f32)
    out_ref[arows, :] = (own_ref[arows, :].astype(f32) + update).astype(bf16)


def layer_kernel(
    idx_ref, nb_ref, cnt_ref, own_ref, place_ref, head_ref, cell_ref, frac_ref, col_ref, row_ref,
    wsrc_ref, wdst_ref, wrad_ref, wmid_ref, wout_ref, wcharge_ref,
    fz0, fz1, fy0, fy1, fx0, fx1, ux0, ux1, uy0, uy1, uz0, uz1,
    new_ref, pot_ref,
    feat_halo, geo_halo, zsend, zrecv, ysend, yrecv, xsend, xrecv, isend, irecv,
    tab_s, src_s, geo_s, ang_s, rad_s, inv_s, grid_s, charge_s, along_s, influence_s,
    feat_send, feat_recv, geo_send, geo_recv, zs_sem, zr_sem, ys_sem, yr_sem, xs_sem, xr_sem, is_sem, ir_sem,
):
    f32, bf16 = jnp.float32, jnp.bfloat16
    me, part = lax.axis_index("dom"), lax.axis_index("sub")
    doms, subs = 64, 4
    turn = lambda x, step, size: lax.rem(x + (step + size), size)

    barrier = pltpu.get_barrier_semaphore()

    def greet(dom, sub):
        pl.semaphore_signal(barrier, inc=1, device_id=(dom, sub), device_id_type=pl.DeviceIdType.MESH)

    for step_x in (-1, 1):
        for step_y in (-1, 1):
            greet(turn(me, step_x, doms), turn(part, step_y, subs))
    for step in range(1, subs):
        greet(me, turn(part, step, subs))

    def greet_dom(step, carry):
        greet(lax.rem(me + step, doms), part)
        return carry

    lax.fori_loop(1, doms, greet_dom, 0)
    pl.semaphore_wait(barrier, 4 + subs - 1 + doms - 1)

    def remote(src, dst, send, recv, dom, sub):
        return pltpu.make_async_remote_copy(
            src_ref=src, dst_ref=dst, send_sem=send, recv_sem=recv,
            device_id=(dom, sub), device_id_type=pl.DeviceIdType.MESH,
        )

    geo_copies = []
    for r, (place_x, place_y) in enumerate(halo_places):
        target = (turn(me, 1 - place_x, doms), turn(part, 1 - place_y, subs))
        geo_copies.append(remote(head_ref, geo_halo.at[r], geo_send.at[r], geo_recv.at[r], *target))

    def feat_copy(src, place_x, place_y):
        r = halo_places.index((place_x, place_y))
        if (place_x, place_y) in ((0, 1), (2, 1)):
            target = (turn(me, 1 - place_x, doms), part)
        else:
            target = (me, turn(part, 1 - place_y, subs))
        return remote(src, feat_halo.at[r], feat_send.at[r], feat_recv.at[r], *target)

    rows = own_ref.at[pl.ds(0, head_rows)]
    first = [feat_copy(rows, 0, 1), feat_copy(rows, 2, 1), feat_copy(rows, 1, 0), feat_copy(rows, 1, 2)]
    slot = lambda x, y: feat_halo.at[halo_places.index((x, y))]
    second = [feat_copy(slot(x, 1), x, y) for x in (0, 2) for y in (0, 2)]
    for copy in geo_copies + first:
        copy.start()

    def swap_sub(src, dst, send, recv):
        return [
            remote(src.at[turn(part, step, subs)], dst.at[part], send.at[step - 1], recv.at[step - 1],
                   me, turn(part, step, subs))
            for step in range(1, subs)
        ]

    def dom_copy(src, dst, send, recv, step):
        target = lax.rem(me + step, doms)
        return remote(src.at[target], dst.at[me], send.at[step - 1], recv.at[step - 1], target, part)

    def swap_dom(src, dst, send, recv):
        def start(step, carry):
            dom_copy(src, dst, send, recv, step).start()
            return carry

        lax.fori_loop(1, doms, start, 0)
        dst[me] = src[me]

    def dom_wait(src, dst, send, recv, which):
        def wait(step, carry):
            getattr(dom_copy(src, dst, send, recv, step), which)()
            return carry

        lax.fori_loop(1, doms, wait, 0)

    charge_s[...] = charge_row(own_ref, wcharge_ref)
    spread(cell_ref, frac_ref, charge_s, along_s, grid_s, (fz0[...], fz1[...]), zsend)
    z_copies = swap_sub(zsend, zrecv, zs_sem, zr_sem)
    for copy in z_copies:
        copy.start()
    zrecv[part] = zsend[part]

    halved = lambda ref: (ref[...].astype(f32) * 0.5).astype(bf16)
    w_src, w_dst, w_mid, w_out = halved(wsrc_ref), halved(wdst_ref), halved(wmid_ref), wout_ref[...]
    wr = wrad_ref[...] * 0.5
    wr_hi = wr.astype(bf16).astype(f32)
    w_ext = jnp.concatenate([wr_hi, wr_hi, wr - wr_hi, jnp.zeros_like(wr)], axis=0).astype(bf16)
    src_s[...] = jnp.dot(own_ref[...], w_src, preferred_element_type=f32)
    tab_s[table_pad : table_pad + 2048, :] = jnp.dot(own_ref[...], w_dst, preferred_element_type=f32)
    tab_s[0:table_pad, :] = jnp.zeros((table_pad, 128), f32)
    tab_s[table_pad + 6144 :, :] = jnp.zeros((table_pad, 128), f32)
    influence_s[...] = influence_block(col_ref, row_ref)
    for copy in geo_copies:
        copy.wait_recv()
    for c in range(3):
        geo_s[c * 48 : c * 48 + 16, :] = place_ref[c * 16 : c * 16 + 16, :]
        for r, (place_x, place_y) in enumerate(halo_places):
            shift = (4.0 * (place_x - 1), 64.0 * (place_y - 1), 0.0)[c]
            at = c * 48 + 16 + r * 4
            geo_s[at : at + 4, :] = geo_halo[r, c * 4 : c * 4 + 4, :] + shift

    def geometry(g, carry):
        geometry_step(2 * g, nb_ref, cnt_ref, geo_s, ang_s, rad_s)
        geometry_step(2 * g + 1, nb_ref, cnt_ref, geo_s, ang_s, rad_s)
        return carry

    lax.fori_loop(0, 6, geometry, 0)
    for copy in first[:2]:
        copy.wait_recv()
    for copy in second:
        copy.start()
    lax.fori_loop(6, 16, geometry, 0)

    for copy in z_copies:
        copy.wait_recv()
    forward_y_step(zrecv, (fy0[...], fy1[...]), ysend)
    swap_dom(ysend, yrecv, ys_sem, yr_sem)

    for copy in first[2:] + second:
        copy.wait_recv()
    for r in range(8):
        base = table_pad + 2048 + r * head_rows
        tab_s[base : base + head_rows, :] = jnp.dot(feat_halo[r], w_dst, preferred_element_type=f32)

    i_copies = swap_sub(isend, irecv, is_sem, ir_sem)

    def edges(g, carry):
        @pl.when(g == edge_split[0])
        def _():
            dom_wait(ysend, yrecv, ys_sem, yr_sem, "wait_recv")
            filter_step(yrecv, (fx0[...], fx1[...]), (ux0[...], ux1[...]), influence_s, xsend)
            swap_dom(xsend, xrecv, xs_sem, xr_sem)

        @pl.when(g == edge_split[1])
        def _():
            dom_wait(xsend, xrecv, xs_sem, xr_sem, "wait_recv")
            inverse_y_step(xrecv, (uy0[...], uy1[...]), isend)
            for copy in i_copies:
                copy.start()
            irecv[part] = isend[part]

        edge_step(g, w_ext, w_mid, w_out, idx_ref, own_ref, tab_s, src_s, ang_s, rad_s, inv_s, new_ref)
        return carry

    lax.fori_loop(0, 32, edges, 0)
    for copy in i_copies:
        copy.wait_recv()
    read_step(irecv, cell_ref, frac_ref, along_s, (uz0[...], uz1[...]), pot_ref, grid_s)
    for copy in geo_copies + first + second + z_copies + i_copies:
        copy.wait_send()
    dom_wait(ysend, yrecv, ys_sem, yr_sem, "wait_send")
    dom_wait(xsend, xrecv, xs_sem, xr_sem, "wait_send")


def local(features, offsets, frac, neighbors, counts, w_src, w_dst, w_rad, w_mid, w_out, w_charge):
    f32, bf16 = jnp.float32, jnp.bfloat16
    own = features[0, 0]
    dom, sub = lax.axis_index("dom"), lax.axis_index("sub")
    anchor = jnp.stack([dom * 4, sub * 64, jnp.zeros_like(dom)]).astype(jnp.int32)
    cells = offsets[:, 0, 0] - anchor[:, None]
    fracs = frac[:, 0, 0]
    place = cells.astype(f32) + fracs
    head = jnp.concatenate([place[:, :head_rows].reshape(12, 128), jnp.zeros((4, 128), f32)], axis=0)

    square, factor = jnp.asarray(wave_square), jnp.asarray(wave_factor)
    pick = lambda table: (table.reshape(4, 64)[:, dom][:, None], table.reshape(4, 64)[sub][None, :])
    square_y, square_z = pick(square)
    factor_y, factor_z = pick(factor)
    row = jnp.stack([(square_y + square_z).reshape(GRID), (factor_y * factor_z).reshape(GRID)])
    col = jnp.stack([square, factor])[:, :, None]

    pairs = neighbors[0, 0]
    operands = (
        pairs.reshape(-1), pairs.reshape(256, 128), counts[0, 0].reshape(16, 128), own, place.reshape(48, 128), head,
        cells, fracs, col, row, w_src, w_dst, w_rad, w_mid, w_out, w_charge[None, :],
        *forward_z, *forward_y, *forward_x, *inverse_x, *inverse_y, *inverse_z,
    )
    vmem = pl.BlockSpec(memory_space=pltpu.VMEM)
    smem = pl.BlockSpec(memory_space=pltpu.SMEM)
    dma = pltpu.SemaphoreType.DMA
    slabs = pltpu.VMEM((4, rows_y, 512), f32)
    pencils = pltpu.VMEM((64, 1, 2048), f32)
    new_rows, potential = pl.pallas_call(
        layer_kernel,
        in_specs=[smem] + [vmem] * (len(operands) - 1),
        out_specs=(vmem, vmem),
        out_shape=(jax.ShapeDtypeStruct((2048, 128), bf16), jax.ShapeDtypeStruct((1, 2048), f32)),
        scratch_shapes=[
            pltpu.VMEM((8, head_rows, 128), bf16), pltpu.VMEM((8, 16, 128), f32),
            slabs, slabs, pencils, pencils, pencils, pencils, slabs, slabs,
            pltpu.VMEM((6144 + 2 * table_pad, 128), f32), pltpu.VMEM((2048, 128), f32), pltpu.VMEM((144, 128), f32),
            pltpu.VMEM((9, 256, 128), f32), pltpu.VMEM((256, 8, 128), f32), pltpu.VMEM((64, 384), f32),
            pltpu.VMEM((ext_x * rows_y, GRID), f32), pltpu.VMEM((8, 2048), f32), pltpu.VMEM((2, GRID, 2048), bf16),
            pltpu.VMEM((GRID, GRID), f32),
            dma((8,)), dma((8,)), dma((8,)), dma((8,)), dma((3,)), dma((3,)),
            dma((63,)), dma((63,)), dma((63,)), dma((63,)), dma((3,)), dma((3,)),
        ],
        compiler_params=pltpu.CompilerParams(
            vmem_limit_bytes=50 * 2**20, collective_id=0, has_side_effects=True
        ),
        name="layer",
    )(*operands)
    return new_rows.reshape(features.shape), potential.reshape(1, 1, 2048)


def solution(mesh):
    placed = (
        P("dom", "sub", None, None),
        P(None, "dom", "sub", None),
        P(None, "dom", "sub", None),
        P("dom", "sub", None, None),
        P("dom", "sub", None),
        P(),
        P(),
        P(),
        P(),
        P(),
        P(),
    )
    return jax.shard_map(
        local,
        mesh=mesh,
        in_specs=placed,
        out_specs=(P("dom", "sub", None, None), P("dom", "sub", None)),
        check_vma=False,
    )
```

time: 162 us -> 115 us (0.71)
  starting transfers between devices: 45.8 us -> 0 us
  Pallas kernels: 79.7 us -> 98.9 us
  waiting for transfers between devices: 14.5 us -> 0 us
  local copies, waits for them, and re-layouts: 17.9 us -> 11.7 us
    all_to_all x4 -> x0, starting transfers between devices: 32.5 us -> none  [swap(): return lax.all_to_all(x, axis, split_axis=0, concat_axis=0, tiled=True)]
    pallas_call x10 -> x1, Pallas kernels: 79.7 us -> 98.9 us  [local(): pl.pallas_call(layer_kernel, in_specs=[smem] + [vmem] * (len(operands) -...]
    ppermute x4 -> x0, waiting for transfers between devices: 14.4 us -> none  [shifted(): return lax.ppermute(x, axis, [(i, (i + step) % size) for i in range(size)])]
    ppermute x4 -> x0, starting transfers between devices: 13.3 us -> none  [shifted(): return lax.ppermute(x, axis, [(i, (i + step) % size) for i in range(size)])]
    unnamed x72 -> x54, local copies, waits for them, and re-layouts: 15.5 us -> 4.36 us
    add x2, local copies, waits for them, and re-layouts: 0.09 us -> 1.84 us  [local(): square_y + square_z]
  transfers between devices with their start and end apart: 8 -> 0, of which waited for: 2 -> 0; matrix products, arithmetic and copies ran while one was open for 2% -> 0% of each run, Pallas kernels for 44% -> 0%
where the time goes in v2:
time: 115 us
  Pallas kernels  98.9 us (86%)
  local copies, waits for them, and re-layouts  11.7 us (10%)
  other arithmetic  3.12 us (3%)
    pallas_call x1, Pallas kernels, local(): pl.pallas_call(layer_kernel, in_specs=[smem] + [vmem] * (len(operands) -...  98.9 us
    unnamed x54, local copies, waits for them, and re-layouts  4.36 us

profile of v2, /device:TPU:1, one launch (start us, length us, event | category | flops | bytes accessed | tf_op | source)
XLA Modules:
  0.0 114.7 jit_solution(7736115706909341519)
XLA Ops:
  0.7 0.0 copy-start.24
  0.7 0.0 copy-start.11
  0.7 0.0 copy-start.12
  0.7 0.0 copy-start.13
  0.8 1.4 %copy.28 = s32[1,1,2048,16]{3,2,1,0:T(8,128)S(1)} copy(s32[1,1,2048,16]{2,3,1,0:T(8,128)} %param.28) | data formatting | bytes 262144 | tf_op args[3]
  2.1 1.0 copy-done.21
  3.1 0.0 copy-start.9
  3.2 0.0 copy-start.10
  3.2 0.3 reshape_squeeze.9.idx_ref
  3.5 0.0 copy-start.2
  3.5 0.0 copy-start.3
  3.5 0.0 copy-start.6
  3.5 1.7 %reshape_squeeze.10.nb_ref = s32[256,128]{1,0:T(8,128)S(1)} reshape(s32[1,1,2048,16]{3,2,1,0:T(8,128)} %copy-done.21) | data formatting | bytes 262144 | tf_op jit(solution)/shard_map/reshape;squeeze | solution.py:485
  5.2 0.0 copy-start.1
  5.2 0.1 pad_add_fusion
  5.3 0.1 sub.16
  5.4 0.1 sub.17
  5.5 0.1 convert_add_fusion.place_ref
  5.6 0.8 bitcast_subtract_fusion.cell_ref
  6.4 0.6 reshape.70
  7.0 0.7 concatenate.3.head_ref
  7.7 1.2 %fusion = (f32[64]{0:T(128)}, f32[64]{0:T(128)}) fusion(f32[4,64]{1,0:T(4,128)S(1)} %copy-done.24, s32[]{:T(128)S(6)} %select_n.9, f32[4,64]{1,0:T(4,128)} %constant.73), kind=kLoop, calls=%fused_computation.12 | loop fusion | bytes 1028 | tf_op jit(solution)/shard_map/add | solution.py:480
  8.9 1.4 %dynamic-slice_reduce_fusion = (f32[4]{0:T(128)S(1)}, f32[4]{0:T(128)}) fusion(f32[4,64]{1,0:T(4,128)} %constant.73, s32[]{:T(128)S(6)} %select_n.8, f32[4,64]{1,0:T(4,128)S(1)} %copy-done.24), kind=kLoop, calls=%fused_computation.6 | loop fusion | bytes 68 | tf_op jit(solution)/shard_map/dynamic_slice | solution.py:477
  10.3 0.7 broadcast_multiply_fusion
  11.0 0.6 mul.40
  11.7 0.7 broadcast_add_fusion
  12.4 0.6 add.52
  13.0 0.7 pad_maximum_fusion.row_ref
  13.9 0.5 copy-done.20
  14.4 98.9 %layer.1 = (bf16[2048,128]{1,0:T(8,128)(2,1)S(1)}, f32[1,2048]{1,0:T(1,128)S(1)}) custom-call(s32[32768]{0:T(1024)S(1)} %reshape_squeeze.9.idx_ref, s32[256,128]{1,0:T(8,128)S(1)} %reshape_squeeze.10.nb_ref, s32[16,128]{1,0:T(8,128)S(1)} %bitcast.26, bf16[2048,128]{1,0:T(8,128)(2,1)S(1)} %bitcast.23, f32[48,128]{1,0:T(8,128)S(1)} %convert_add_fusion.place_ref, ...), custom_call_target="tpu_custom_call" | custom-call | tf_op jit(solution)/shard_map/layer/pallas_call | solution.py:494
  113.3 0.8 copy.37
  114.1 0.6 copy.38
  (40 shorter events, 0.1 us)
Async XLA Ops:
  0.6 4.8 %copy-start.22 = (f32[3,1,1,2048]{3,2,1,0:T(1,128)S(1)}, f32[3,1,1,2048]{3,2,1,0:T(1,128)}, u32[]{:S(2)}) copy-start(f32[3,1,1,2048]{3,2,1,0:T(1,128)} %param.27) | copy-start | bytes 73732
  0.6 4.8 %copy-start.23 = (s32[3,1,1,2048]{3,2,1,0:T(1,128)S(1)}, s32[3,1,1,2048]{3,2,1,0:T(1,128)}, u32[]{:S(2)}) copy-start(s32[3,1,1,2048]{3,2,1,0:T(1,128)} %param.26) | copy-start | bytes 73732
  0.7 7.0 %copy-start.24 = (f32[4,64]{1,0:T(4,128)S(1)}, f32[4,64]{1,0:T(4,128)}, u32[]{:S(2)}) copy-start(f32[4,64]{1,0:T(4,128)} %constant.72) | copy-start | bytes 3076
  0.7 13.1 %copy-start.11 = (bf16[256,256]{1,0:T(8,128)(2,1)S(1)}, bf16[256,256]{1,0:T(8,128)(2,1)}, u32[]{:S(2)}) copy-start(bf16[256,256]{1,0:T(8,128)(2,1)} %constant.50.clone.fz1) | copy-start | bytes 393220
  0.7 13.1 %copy-start.12 = (bf16[256,256]{1,0:T(8,128)(2,1)S(1)}, bf16[256,256]{1,0:T(8,128)(2,1)}, u32[]{:S(2)}) copy-start(bf16[256,256]{1,0:T(8,128)(2,1)} %constant.59.clone.uz0) | copy-start | bytes 393220
  0.7 13.1 %copy-start.13 = (bf16[256,256]{1,0:T(8,128)(2,1)S(1)}, bf16[256,256]{1,0:T(8,128)(2,1)}, u32[]{:S(2)}) copy-start(bf16[256,256]{1,0:T(8,128)(2,1)} %constant.60.clone.uz1) | copy-start | bytes 393220
  0.7 13.1 %copy-start.15 = (bf16[128,128]{1,0:T(8,128)(2,1)S(1)}, bf16[128,128]{1,0:T(8,128)(2,1)}, u32[]{:S(2)}) copy-start(bf16[128,128]{1,0:T(8,128)(2,1)} %wsrc_ref.1) | copy-start | bytes 98308
  0.7 13.1 %copy-start.16 = (bf16[128,128]{1,0:T(8,128)(2,1)S(1)}, bf16[128,128]{1,0:T(8,128)(2,1)}, u32[]{:S(2)}) copy-start(bf16[128,128]{1,0:T(8,128)(2,1)} %wdst_ref.1) | copy-start | bytes 98308
  0.7 13.1 %copy-start.17 = (bf16[128,128]{1,0:T(8,128)(2,1)S(1)}, bf16[128,128]{1,0:T(8,128)(2,1)}, u32[]{:S(2)}) copy-start(bf16[128,128]{1,0:T(8,128)(2,1)} %wmid_ref.1) | copy-start | bytes 98308
  0.7 13.1 %copy-start.18 = (s32[1,1,2048]{2,1,0:T(1,128)S(1)}, s32[1,1,2048]{2,1,0:T(1,128)}, u32[]{:S(2)}) copy-start(s32[1,1,2048]{2,1,0:T(1,128)} %param.29) | copy-start | bytes 24580
  0.7 13.1 %copy-start.19 = (f32[8,128]{1,0:T(8,128)S(1)}, f32[8,128]{1,0:T(8,128)}, u32[]{:S(2)}) copy-start(f32[8,128]{1,0:T(8,128)} %wrad_ref.1) | copy-start | bytes 12292
  2.1 1.0 copy-start.21
  3.1 10.7 %copy-start.4 = (bf16[448,256]{1,0:T(8,128)(2,1)S(1)}, bf16[448,256]{1,0:T(8,128)(2,1)}, u32[]{:S(2)}) copy-start(bf16[448,256]{1,0:T(8,128)(2,1)} %constant.55.clone.ux0) | copy-start | bytes 688132
  3.1 10.7 %copy-start.5 = (bf16[448,256]{1,0:T(8,128)(2,1)S(1)}, bf16[448,256]{1,0:T(8,128)(2,1)}, u32[]{:S(2)}) copy-start(bf16[448,256]{1,0:T(8,128)(2,1)} %constant.56.clone.ux1) | copy-start | bytes 688132
  3.1 10.7 %copy-start.7 = (bf16[256,288]{1,0:T(8,128)(2,1)S(1)}, bf16[256,288]{1,0:T(8,128)(2,1)}, u32[]{:S(2)}) copy-start(bf16[256,288]{1,0:T(8,128)(2,1)} %constant.52.clone.fy1) | copy-start | bytes 442372
  3.1 10.7 %copy-start.8 = (bf16[288,256]{1,0:T(8,128)(2,1)S(1)}, bf16[288,256]{1,0:T(8,128)(2,1)}, u32[]{:S(2)}) copy-start(bf16[288,256]{1,0:T(8,128)(2,1)} %constant.57.clone.uy0) | copy-start | bytes 442372
  3.1 10.7 %copy-start.9 = (bf16[288,256]{1,0:T(8,128)(2,1)S(1)}, bf16[288,256]{1,0:T(8,128)(2,1)}, u32[]{:S(2)}) copy-start(bf16[288,256]{1,0:T(8,128)(2,1)} %constant.58.clone.uy1) | copy-start | bytes 442372
  3.2 10.7 %copy-start.10 = (bf16[256,256]{1,0:T(8,128)(2,1)S(1)}, bf16[256,256]{1,0:T(8,128)(2,1)}, u32[]{:S(2)}) copy-start(bf16[256,256]{1,0:T(8,128)(2,1)} %constant.49.clone.fz0) | copy-start | bytes 393220
  3.2 10.7 %copy-start.14 = (bf16[384,128]{1,0:T(8,128)(2,1)S(1)}, bf16[384,128]{1,0:T(8,128)(2,1)}, u32[]{:S(2)}) copy-start(bf16[384,128]{1,0:T(8,128)(2,1)} %wout_ref.1) | copy-start | bytes 294916
  3.5 10.4 %copy-start = (bf16[1,1,2048,128]{3,2,1,0:T(8,128)(2,1)S(1)}, bf16[1,1,2048,128]{3,2,1,0:T(8,128)(2,1)}, u32[]{:S(2)}) copy-start(bf16[1,1,2048,128]{3,2,1,0:T(8,128)(2,1)} %param.25) | copy-start | bytes 1572868
  3.5 10.4 %copy-start.2 = (bf16[256,448]{1,0:T(8,128)(2,1)S(1)}, bf16[256,448]{1,0:T(8,128)(2,1)}, u32[]{:S(2)}) copy-start(bf16[256,448]{1,0:T(8,128)(2,1)} %constant.53.clone.fx0) | copy-start | bytes 688132
  3.5 10.4 %copy-start.3 = (bf16[256,448]{1,0:T(8,128)(2,1)S(1)}, bf16[256,448]{1,0:T(8,128)(2,1)}, u32[]{:S(2)}) copy-start(bf16[256,448]{1,0:T(8,128)(2,1)} %constant.54.clone.fx1) | copy-start | bytes 688132
  3.5 10.4 %copy-start.6 = (bf16[256,288]{1,0:T(8,128)(2,1)S(1)}, bf16[256,288]{1,0:T(8,128)(2,1)}, u32[]{:S(2)}) copy-start(bf16[256,288]{1,0:T(8,128)(2,1)} %constant.51.clone.fy0) | copy-start | bytes 442372
  5.2 8.7 %copy-start.1 = (f32[2,256,1]{2,1,0:T(8,128)S(1)}, f32[2,256,1]{2,1,0:T(8,128)}, u32[]{:S(2)}) copy-start(f32[2,256,1]{2,1,0:T(8,128)} %constant.71.col_ref) | copy-start | bytes 6148
  13.8 0.7 copy-start.20

commit v3 on v2

v3 whole, which is shorter than its diff:
```python
import functools
import math

import jax
import jax.numpy as jnp
import ml_dtypes
import numpy as np
from jax import lax
from jax.experimental import pallas as pl
from jax.experimental.pallas import tpu as pltpu
from jax.sharding import PartitionSpec as P

GRID = 256
ext_x = 7
ext_y = 67
rows_y = 72
rows_back = 80
head_rows = 512
table_pad = 8
edge_split = (6, 11)
halo_places = [(0, 0), (0, 1), (0, 2), (1, 0), (1, 2), (2, 0), (2, 1), (2, 2)]


def split_table(table):
    high = table.astype(ml_dtypes.bfloat16)
    low = (table - high.astype(np.float64)).astype(ml_dtypes.bfloat16)
    return high, low


def real_basis():
    cells = np.arange(GRID)
    basis = np.zeros((GRID, GRID))
    for k in range(GRID):
        wave = k if k <= GRID // 2 else k - GRID // 2
        angle = 2.0 * np.pi / GRID * ((wave * cells) % GRID)
        scale = math.sqrt((1.0 if k in (0, GRID // 2) else 2.0) / GRID)
        basis[k] = scale * (np.cos(angle) if k <= GRID // 2 else np.sin(angle))
    return basis


def wave_tables():
    index = np.arange(GRID)
    wave = np.where(index <= GRID // 2, index, index - GRID // 2) / GRID
    factor = (2.0 + np.cos(2.0 * np.pi * wave)) / 3.0
    return (wave**2).astype(np.float32), (1.0 / factor**2).astype(np.float32)


basis = real_basis()
columns_y = np.zeros((GRID, 4 * rows_y))
for c in range(4):
    for y in range(ext_y):
        columns_y[:, c * rows_y + y] = basis[:, (64 * c - 1 + y) % GRID]
columns_x = np.concatenate([basis[:, (4 * np.arange(64) - 1 + x) % GRID] for x in range(ext_x)], axis=1)
forward_z = split_table(basis.T.copy())
inverse_z = split_table(basis)
forward_y = split_table(columns_y)
lines_y = np.zeros((4 * rows_back, GRID))
for c in range(4):
    lines_y[c * rows_back : c * rows_back + ext_y] = columns_y[:, c * rows_y : c * rows_y + ext_y].T
inverse_y = split_table(lines_y)
forward_x = split_table(columns_x)
inverse_x = split_table(columns_x.T.copy())
wave_square, wave_factor = wave_tables()
waves = np.stack([wave_square, wave_factor])
wave_x = np.repeat(waves.reshape(2 * GRID, 1), 128, axis=1)
wave_yz = np.concatenate(
    [np.repeat(waves.reshape(2, 4, 64).transpose(0, 2, 1), 64, axis=2), np.tile(waves.reshape(2, 4, 64), (1, 1, 4)), np.zeros((2, 4, GRID), np.float32)], axis=1
).reshape(144, GRID)
narrow = np.concatenate([*forward_z, *inverse_z, *inverse_x, *inverse_y], axis=0)
wide = np.concatenate([np.pad(t, ((0, 0), (0, 512 - t.shape[1]))) for t in (*forward_y, *forward_x)], axis=0)

def halves(x):
    high = x.astype(jnp.bfloat16)
    return high, (x - high.astype(jnp.float32)).astype(jnp.bfloat16)


def dot_split(a, b, pattern=(((1,), (0,)), ((), ()))):
    dot = functools.partial(lax.dot_general, dimension_numbers=pattern, preferred_element_type=jnp.float32)
    return dot(a[0], b[0]) + (dot(a[0], b[1]) + dot(a[1], b[0]))


def spline_four(f):
    g = 1.0 - f
    f2 = f * f
    f3 = f2 * f
    return (
        g * g * g * (1.0 / 6.0),
        (3.0 * f3 - 6.0 * f2 + 4.0) * (1.0 / 6.0),
        (-3.0 * f3 + 3.0 * f2 + 3.0 * f + 1.0) * (1.0 / 6.0),
        f3 * (1.0 / 6.0),
    )


def placed_weights(count, cell, f, wraps=False):
    ids = lax.broadcasted_iota(jnp.int32, (count, cell.shape[1]), 0)
    step = ids - cell
    if wraps:
        step = (step + 1) & (GRID - 1)
    result = jnp.zeros(step.shape, jnp.float32)
    for k, weight in enumerate(spline_four(f)):
        result = jnp.where(step == k, weight, result)
    return result


def pair_tiles(first, second, half):
    lane = lax.broadcasted_iota(jnp.int32, first.shape, 1)
    if half == 0:
        return jnp.where(lane < 64, first, pltpu.roll(second, 64, 1))
    return jnp.where(lane < 64, pltpu.roll(first, 64, 1), second)


def charge_row(feat_ref, w_ref):
    f32, bf16 = jnp.float32, jnp.bfloat16
    w = jnp.broadcast_to(w_ref[...], (16, 128))
    top = w.astype(bf16).astype(f32)
    mid = (w - top).astype(bf16).astype(f32)
    sub = lax.broadcasted_iota(jnp.int32, (16, 128), 0)
    parts = jnp.where(sub == 0, top, jnp.where(sub == 1, mid, jnp.where(sub == 2, w - top - mid, 0.0))).astype(bf16)
    raw = lax.dot_general(parts, feat_ref[...], (((1,), (1,)), ((), ())), preferred_element_type=f32)
    raw = jnp.broadcast_to(raw[0:1] + raw[1:2] + raw[2:3], (8, raw.shape[1]))
    lane = lax.broadcasted_iota(jnp.int32, raw.shape, 1)
    mate = jnp.where(lane % 2 == 0, pltpu.roll(raw, raw.shape[1] - 1, 1), pltpu.roll(raw, 1, 1))
    return 0.5 * (raw - mate)


def atom_row(ref, c, i):
    return jnp.concatenate([ref[pl.ds(c * 16 + 4 * i + q, 1), :] for q in range(4)], axis=1)


def spread(cell_ref, frac_ref, charge_s, along_s, grid_s, table, out_ref):
    grid_s[...] = jnp.zeros_like(grid_s)

    def tile(i, carry):
        cols = pl.ds(pl.multiple_of(i * 512, 512), 512)
        along_x = placed_weights(8, atom_row(cell_ref, 0, i), atom_row(frac_ref, 0, i)) * charge_s[0:1, cols]
        along_y = placed_weights(rows_y, atom_row(cell_ref, 1, i), atom_row(frac_ref, 1, i))
        along_z = halves(placed_weights(GRID, atom_row(cell_ref, 2, i), atom_row(frac_ref, 2, i), True))
        along_s[0, :, cols] = along_z[0]
        along_s[1, :, cols] = along_z[1]
        plane = jnp.concatenate([along_x[x : x + 1] * along_y for x in range(ext_x)], axis=0)
        grid_s[...] += dot_split(halves(plane), along_z, (((1,), (1,)), ((), ())))
        return carry

    lax.fori_loop(0, 4, tile, 0)
    waves = dot_split(halves(grid_s[...]), table)
    for c in range(4):
        cols = slice(128 * (c // 2), 128 * (c // 2) + 128)
        slab = lambda x: waves[x * rows_y : (x + 1) * rows_y, cols]
        for q in range(3):
            out_ref[c, q * rows_y : (q + 1) * rows_y, :] = pair_tiles(slab(2 * q), slab(2 * q + 1), c % 2)
        last = slab(6)
        below = jnp.concatenate([last[40:rows_y], jnp.zeros((8, 128), jnp.float32)], axis=0)
        out_ref[c, 3 * rows_y : 3 * rows_y + 40, :] = pair_tiles(last[0:40], below, c % 2)


def forward_y_step(x_ref, table, out_ref):
    pieces = []
    for c in range(4):
        tail = x_ref[c, 3 * rows_y :, :]
        last = jnp.concatenate([tail, pltpu.roll(tail, 64, 1)[0 : rows_y - 40]], axis=0)
        pieces.append(jnp.concatenate([x_ref[c, q * rows_y : (q + 1) * rows_y, :] for q in range(3)] + [last], axis=1))
    waves = dot_split(table, halves(jnp.concatenate(pieces, axis=0)))
    for j in range(4):
        out_ref[:, 0, j * 384 : j * 384 + 384] = waves[64 * j : 64 * j + 64, 0:384]
    for p in range(2):
        tail = [waves[128 * p + 64 * q : 128 * p + 64 * q + 64, 384:512] for q in range(2)]
        out_ref[:, 0, 1536 + p * 128 : 1664 + p * 128] = pair_tiles(tail[0], tail[1], 0)


def influence_block(x_ref, yz_ref, me, part):
    spot = lambda row: yz_ref[pl.ds(row, 1), :]
    twice = lambda block: jnp.concatenate([block, block], axis=1)
    square = twice(x_ref[0:GRID, :]) + (spot(me) + spot(64 + part))
    factor = twice(x_ref[GRID:, :]) * (spot(72 + me) * spot(136 + part))
    positive = square > 0.0
    safe = jnp.where(positive, square, 1.0)
    return jnp.where(positive, 16.0 * jnp.exp(square * (-(math.pi**2))) / safe * factor, 0.0)


def filter_step(x_ref, table, back, influence_ref, turn_s, out_ref):
    pieces = []
    for x in range(ext_x - 1):
        slabs = [x_ref[:, 0, j * 384 + 128 * (x // 2) : j * 384 + 128 * (x // 2) + 128] for j in range(4)]
        pieces.append(jnp.concatenate([pair_tiles(slabs[2 * p], slabs[2 * p + 1], x % 2) for p in range(2)], axis=1))
    pieces.append(x_ref[:, 0, 1536:1792])
    waves = dot_split(table, halves(jnp.concatenate(pieces, axis=0)))
    cells = dot_split(back, halves(waves * influence_ref[...]))
    for j in range(4):
        for q in range(4):
            cols = slice(128 * (j // 2), 128 * (j // 2) + 128)
            first = cells[128 * q : 128 * q + 64, cols]
            if 2 * q + 1 < ext_x:
                second = cells[128 * q + 64 : 128 * q + 128, cols]
            else:
                second = jnp.zeros_like(first)
            turn_s[:, j * 4 + q, :] = pair_tiles(first, second, j % 2)
    out_ref[...] = turn_s[...].astype(jnp.bfloat16)


def inverse_y_step(x_ref, table, turn_s, out_ref):
    turn_s[...] = x_ref[...].astype(jnp.float32)
    data = jnp.concatenate(
        [jnp.concatenate([turn_s[:, j * 4 + q, :] for q in range(4)], axis=1) for j in range(4)], axis=0
    ).astype(jnp.bfloat16)
    dot = functools.partial(jnp.dot, preferred_element_type=jnp.float32)
    cells = dot(table[0], data) + dot(table[1], data)
    for c in range(4):
        out_ref[c] = cells[c * rows_back : (c + 1) * rows_back].astype(jnp.bfloat16)


def read_step(x_ref, cell_ref, frac_ref, along_s, table, out_ref, grid_s):
    f32 = jnp.float32
    pieces = []
    for x in range(ext_x):
        cols = slice(128 * (x // 2), 128 * (x // 2) + 128)
        slab = [x_ref[c, :, cols].astype(f32) for c in range(4)]
        pieces.append(jnp.concatenate([pair_tiles(slab[2 * p], slab[2 * p + 1], x % 2) for p in range(2)], axis=1))
    lines = jnp.concatenate(pieces, axis=0).astype(jnp.bfloat16)
    dot = functools.partial(jnp.dot, preferred_element_type=f32)
    grid_s[...] = dot(lines, table[0]) + dot(lines, table[1])

    def tile(i, carry):
        cols = pl.ds(pl.multiple_of(i * 512, 512), 512)
        along_x = placed_weights(8, atom_row(cell_ref, 0, i), atom_row(frac_ref, 0, i))
        along_y = placed_weights(rows_back, atom_row(cell_ref, 1, i), atom_row(frac_ref, 1, i))
        lines = dot_split(halves(grid_s[...]), (along_s[0, :, cols], along_s[1, :, cols]))
        total = jnp.zeros(along_y.shape, f32)
        for x in range(ext_x):
            total = total + along_x[x : x + 1] * lines[x * rows_back : (x + 1) * rows_back]
        out_ref[:, cols] = jnp.sum(total * along_y, axis=0, keepdims=True)
        return carry

    lax.fori_loop(0, 4, tile, 0)


def geometry_step(g, nb_ref, cnt_ref, geo_s, ang_s, rad_s):
    f32 = jnp.float32
    sub = lax.broadcasted_iota(jnp.int32, (8, 128), 0)
    lane = lax.broadcasted_iota(jnp.int32, (8, 128), 1)
    rows = pl.ds(pl.multiple_of(g * 8, 8), 8)
    nb = nb_ref[rows, :]
    low = nb & 127
    high = nb >> 7
    part = [jnp.zeros((8, 128), f32) for _ in range(3)]
    for h in range(48):
        hit = high == h
        for c in range(3):
            row = jnp.broadcast_to(geo_s[c * 48 + h : c * 48 + h + 1, :], (8, 128))
            part[c] = jnp.where(hit, jnp.take_along_axis(row, low, axis=1), part[c])
    centre = (g % 2) * 64 + sub * 8 + lane // 16
    spot = lambda ref, row: jnp.take_along_axis(jnp.broadcast_to(ref[pl.ds(row, 1), :], (8, 128)), centre, axis=1)
    mine = [spot(geo_s, c * 48 + g // 2) for c in range(3)]
    live = spot(cnt_ref, g // 2)
    dx = part[0] - mine[0]
    dy = part[1] - mine[1]
    dz = part[2] - mine[2]
    cells = jnp.floor(part[2]) - jnp.floor(mine[2])
    dz = jnp.where(cells >= 128.0, dz - 256.0, jnp.where(cells < -128.0, dz + 256.0, dz))
    squared = dx * dx + dy * dy + dz * dz + 1.0
    distance = jnp.sqrt(squared)
    inverse = 1.0 / distance
    nx, ny, nz = dx * inverse, dy * inverse, dz * inverse
    env = jnp.where((lane % 16) < live, 1.0 / (1.0 + squared * (1.0 / 4096.0)), 0.0)
    r3, r5, r15 = math.sqrt(3.0), math.sqrt(5.0), math.sqrt(15.0)
    ex, ey, ez = env * nx, env * ny, env * nz
    angular = [
        env, r3 * ex, r3 * ey, r3 * ez, r15 * ex * ny, r15 * ey * nz,
        (0.5 * r5) * (3.0 * ez * nz - env), r15 * ex * nz, (0.5 * r15) * (ex * nx - ey * ny),
    ]
    for m in range(9):
        ang_s[m, rows, :] = angular[m]
    for j in range(8):
        rad_s[rows, j, :] = jnp.exp(distance * (-1.0 / 2.0**j))


def gather_rows(g, r, idx_ref, tab_s, buf):
    sub = lax.broadcasted_iota(jnp.int32, (8, 128), 0)
    for t in range(r*16, r*16+16):
        acc = None
        for j in range(8):
            v = tab_s[pl.ds(idx_ref[g * 1024 + (t * 8 + j)] + (table_pad - j), 8), :]
            acc = v if acc is None else jnp.where(sub == j, v, acc)
        buf[t*8:t*8+8,:] = acc


def moments_pair(g, p, hid, ang_s, inv_all):
    f32, bf16 = jnp.float32, jnp.bfloat16
    sub = lax.broadcasted_iota(jnp.int32, (8, 128), 0)
    diag = (lax.broadcasted_iota(jnp.int32, (8, 128), 1) // 16) == sub
    zero = jnp.zeros((8, 128), f32)
    blocks_hi, blocks_lo = [], []
    for m in range(9):
        cols_hi, cols_lo = [], []
        for q in range(2):
            line = ang_s[m, pl.ds(g * 8 + (2 * p + q), 1), :]
            row = jnp.where(diag, jnp.broadcast_to(line, (8, 128)), 0.0)
            row_hi = row.astype(bf16).astype(f32)
            row_lo = row - row_hi
            cols_hi.append(jnp.concatenate([row_hi, zero] if q == 0 else [zero, row_hi], axis=0).astype(bf16))
            cols_lo.append(jnp.concatenate([row_lo, zero] if q == 0 else [zero, row_lo], axis=0).astype(bf16))
        blocks_hi.append(jnp.concatenate(cols_hi, axis=1))
        blocks_lo.append(jnp.concatenate(cols_lo, axis=1))
    both = jnp.concatenate(blocks_hi + blocks_lo, axis=0)
    mom2 = jnp.dot(both, hid, preferred_element_type=f32)
    mom = mom2[:144, :128] + mom2[:144, 128:] + mom2[144:, :128]
    sq = [mom[m * 16 : m * 16 + 16] ** 2 for m in range(9)]
    inv = jnp.concatenate([sq[0], sq[1] + sq[2] + sq[3], (sq[4] + sq[5]) + (sq[6] + sq[7]) + sq[8]], axis=1)
    inv_all[pl.ds(pl.multiple_of(g*64 + p*16,16),16), :] = inv.astype(bf16)


def edge_pipe(g, nxt, w_ext, w_mid, idx_ref, tab_s, src_s, ang_s, rad_s, buf, other, inv_all):
    f32, bf16 = jnp.float32, jnp.bfloat16
    pieces = []
    for r in range(8):
        rad = rad_s[g * 8 + r]
        rad_hi = rad.astype(bf16).astype(f32)
        pieces.append(jnp.concatenate([rad_hi, rad - rad_hi, rad_hi, jnp.zeros_like(rad)], axis=0).astype(bf16))
    rad_ext = jnp.concatenate(pieces, axis=1)
    term = lax.dot_general(rad_ext, w_ext, (((0,), (0,)), ((), ())), preferred_element_type=f32)
    lats = []
    for r in range(8):
        if nxt is not None:
            gather_rows(nxt, r, idx_ref, tab_s, other)
        src = src_s[pl.ds(pl.multiple_of(g * 64 + r*8, 8), 8), :]
        src = jnp.broadcast_to(src[:, None, :], (8, 16, 128)).reshape(128, 128)
        half = buf[r*128:r*128+128,:] + src + term[r*128:r*128+128]
        lats.append((half + half * jnp.tanh(half)).astype(bf16))
    half = jnp.dot(jnp.concatenate(lats, axis=0), w_mid, preferred_element_type=f32)
    hidden = half + half * jnp.tanh(half)
    hid = jnp.concatenate(halves(hidden), axis=1)
    for p in range(4):
        moments_pair(g, p, hid[p*256:p*256+256], ang_s, inv_all)


def finish(out_ref, own_ref, inv_all, w_out):
    def step(i, carry):
        rows = pl.ds(pl.multiple_of(i*512,512),512)
        out_ref[rows,:] = (own_ref[rows,:].astype(jnp.float32) + jnp.dot(inv_all[rows,:], w_out, preferred_element_type=jnp.float32)).astype(jnp.bfloat16)
        return carry
    lax.fori_loop(0, 4, step, 0)


def layer_kernel(
    idx_ref, own_hbm, nb_hbm, cnt_hbm, offset_hbm, frac_hbm, wcharge_hbm, wsrc_hbm, wdst_hbm, wrad_hbm, wmid_hbm,
    wout_hbm, narrow_hbm, wide_hbm, wave_x_hbm, wave_yz_hbm,
    new_ref, pot_ref,
    feat_halo, geo_halo, zsend, zrecv, ysend, yrecv, xsend, xrecv, isend, irecv,
    tab_s, src_s, geo_s, ang_s, rad_s, inv_s, grid_s, charge_s, along_s, influence_s,
    cell_s, head_s, even_s, odd_s, turn_s, back_s,
    own_ref, nb_ref, cnt_ref, offset_ref, frac_ref, wcharge_ref, wsrc_ref, wdst_ref, wrad_ref, wmid_ref,
    wout_ref, narrow_ref, wide_ref, wave_x_ref, wave_yz_ref, load_sem,
    feat_send, feat_recv, geo_send, geo_recv, zs_sem, zr_sem, ys_sem, yr_sem, xs_sem, xr_sem, is_sem, ir_sem,
):
    f32, bf16 = jnp.float32, jnp.bfloat16
    me, part = lax.axis_index("dom"), lax.axis_index("sub")
    doms, subs = 64, 4
    turn = lambda x, step, size: lax.rem(x + (step + size), size)

    sources = (
        offset_hbm, frac_hbm, own_hbm, wcharge_hbm, narrow_hbm, wsrc_hbm, wdst_hbm, wave_x_hbm, wave_yz_hbm,
        nb_hbm, cnt_hbm, wide_hbm, wrad_hbm, wmid_hbm, wout_hbm,
    )
    places = (
        offset_ref, frac_ref, own_ref, wcharge_ref, narrow_ref, wsrc_ref, wdst_ref, wave_x_ref, wave_yz_ref,
        nb_ref, cnt_ref, wide_ref, wrad_ref, wmid_ref, wout_ref,
    )
    loads = [pltpu.make_async_copy(a, b, load_sem.at[k]) for k, (a, b) in enumerate(zip(sources, places))]
    for load in loads:
        load.start()
    table = lambda at, count: (narrow_ref[at : at + count, :], narrow_ref[at + count : at + 2 * count, :])
    broad = lambda at, width: (wide_ref[at : at + GRID, 0:width], wide_ref[at + GRID : at + 2 * GRID, 0:width])

    barrier = pltpu.get_barrier_semaphore()

    def greet(dom, sub):
        pl.semaphore_signal(barrier, inc=1, device_id=(dom, sub), device_id_type=pl.DeviceIdType.MESH)

    for step_x in (-1, 1):
        for step_y in (-1, 1):
            greet(turn(me, step_x, doms), turn(part, step_y, subs))
    for step in range(1, subs):
        greet(me, turn(part, step, subs))

    def greet_dom(step, carry):
        greet(lax.rem(me + step, doms), part)
        return carry

    lax.fori_loop(1, doms, greet_dom, 0)
    for load in loads[:4]:
        load.wait()
    for c, anchor in enumerate((me * 4, part * 64, 0)):
        cell_s[c * 16 : c * 16 + 16, :] = offset_ref[c * 16 : c * 16 + 16, :] - anchor
        place = cell_s[c * 16 : c * 16 + 16, :].astype(f32) + frac_ref[c * 16 : c * 16 + 16, :]
        geo_s[c * 48 : c * 48 + 16, :] = place
        head_s[c * 4 : c * 4 + 4, :] = place[0:4]
    head_s[12:16, :] = jnp.zeros((4, 128), f32)

    charge_s[...] = charge_row(own_ref, wcharge_ref)
    pl.semaphore_wait(barrier, 4 + subs - 1 + doms - 1)

    def remote(src, dst, send, recv, dom, sub):
        return pltpu.make_async_remote_copy(
            src_ref=src, dst_ref=dst, send_sem=send, recv_sem=recv,
            device_id=(dom, sub), device_id_type=pl.DeviceIdType.MESH,
        )

    geo_copies = []
    for r, (place_x, place_y) in enumerate(halo_places):
        target = (turn(me, 1 - place_x, doms), turn(part, 1 - place_y, subs))
        geo_copies.append(remote(head_s, geo_halo.at[r], geo_send.at[r], geo_recv.at[r], *target))

    odd, high = lax.rem(part, 2), part // 2
    mate, cross = part + 1 - 2 * odd, turn(part, 2 * odd - 1, subs)
    mate_y, cross_y = 2 * odd, 2 - 2 * odd
    rows = own_ref.at[pl.ds(0, head_rows)]

    def feat_copy(k, src, slot, dom, sub):
        return remote(src, feat_halo.at[slot], feat_send.at[k], feat_recv.at[slot], dom, sub)

    def feat_wait(slot):
        remote(rows, feat_halo.at[slot], feat_send.at[0], feat_recv.at[slot], turn(me, 1, doms), part).wait_recv()

    first = [
        feat_copy(0, rows, 1, turn(me, 1, doms), part),
        feat_copy(1, rows, 7, turn(me, -1, doms), part),
        feat_copy(2, rows, 3 + cross_y, me, cross),
        feat_copy(3, rows, 6 * (1 - high) + cross_y, turn(me, 2 * high - 1, doms), cross),
        feat_copy(4, rows, 3 + mate_y, me, mate),
    ]
    second = [
        feat_copy(5, feat_halo.at[6 * high + 1], 6 * high + cross_y, me, cross),
        feat_copy(6, feat_halo.at[1], mate_y, me, mate),
        feat_copy(7, feat_halo.at[7], 6 + mate_y, me, mate),
    ]
    for copy in geo_copies + first:
        copy.start()

    def swap_sub(src, dst, send, recv):
        return [
            remote(src.at[turn(part, step, subs)], dst.at[part], send.at[step - 1], recv.at[step - 1],
                   me, turn(part, step, subs))
            for step in range(1, subs)
        ]

    def dom_copy(src, dst, send, recv, step):
        target = lax.rem(me + step, doms)
        return remote(src.at[target], dst.at[me], send.at[step - 1], recv.at[step - 1], target, part)

    def swap_dom(src, dst, send, recv):
        def start(step, carry):
            dom_copy(src, dst, send, recv, step).start()
            return carry

        lax.fori_loop(1, doms, start, 0)
        dst[me] = src[me]

    def dom_wait(src, dst, send, recv, which):
        def wait(step, carry):
            getattr(dom_copy(src, dst, send, recv, step), which)()
            return carry

        lax.fori_loop(1, doms, wait, 0)

    loads[4].wait()
    spread(cell_s, frac_ref, charge_s, along_s, grid_s, table(0, GRID), zsend)
    z_copies = swap_sub(zsend, zrecv, zs_sem, zr_sem)
    for copy in z_copies:
        copy.start()
    zrecv[part] = zsend[part]

    for load in loads[5:]:
        load.wait()
    halved = lambda ref: (ref[...].astype(f32) * 0.5).astype(bf16)
    w_src, w_dst, w_mid, w_out = halved(wsrc_ref), halved(wdst_ref), halved(wmid_ref), wout_ref[...]
    wr = wrad_ref[...] * 0.5
    wr_hi = wr.astype(bf16).astype(f32)
    w_ext = jnp.concatenate([wr_hi, wr_hi, wr - wr_hi, jnp.zeros_like(wr)], axis=0).astype(bf16)
    src_s[...] = jnp.dot(own_ref[...], w_src, preferred_element_type=f32)
    tab_s[table_pad : table_pad + 2048, :] = jnp.dot(own_ref[...], w_dst, preferred_element_type=f32)
    tab_s[0:table_pad, :] = jnp.zeros((table_pad, 128), f32)
    tab_s[table_pad + 6144 :, :] = jnp.zeros((table_pad, 128), f32)
    feat_wait(1)
    feat_wait(7)
    for copy in second:
        copy.start()
    influence_s[...] = influence_block(wave_x_ref, wave_yz_ref, me, part)
    for copy in geo_copies:
        copy.wait_recv()
    for c in range(3):
        for r, (place_x, place_y) in enumerate(halo_places):
            shift = (4.0 * (place_x - 1), 64.0 * (place_y - 1), 0.0)[c]
            at = c * 48 + 16 + r * 4
            geo_s[at : at + 4, :] = geo_halo[r, c * 4 : c * 4 + 4, :] + shift

    def geometry(g, carry):
        geometry_step(2 * g, nb_ref, cnt_ref, geo_s, ang_s, rad_s)
        geometry_step(2 * g + 1, nb_ref, cnt_ref, geo_s, ang_s, rad_s)
        return carry

    lax.fori_loop(0, 16, geometry, 0)

    for copy in z_copies:
        copy.wait_recv()
    forward_y_step(zrecv, broad(0, 4 * rows_y), ysend)
    swap_dom(ysend, yrecv, ys_sem, yr_sem)

    for slot in (0, 2, 3, 5, 6, 8):
        feat_wait(slot)
    for r, (place_x, place_y) in enumerate(halo_places):
        base = table_pad + 2048 + r * head_rows
        tab_s[base : base + head_rows, :] = jnp.dot(feat_halo[3 * place_x + place_y], w_dst, preferred_element_type=f32)

    i_copies = swap_sub(isend, irecv, is_sem, ir_sem)

    pipe = functools.partial(
        edge_pipe, w_ext=w_ext, w_mid=w_mid, idx_ref=idx_ref, tab_s=tab_s, src_s=src_s, ang_s=ang_s, rad_s=rad_s,
        inv_all=inv_s,
    )
    for r in range(8):
        gather_rows(0, r, idx_ref, tab_s, even_s)

    def edges(i, carry):
        @pl.when(i == edge_split[0])
        def _():
            dom_wait(ysend, yrecv, ys_sem, yr_sem, "wait_recv")
            filter_step(yrecv, broad(2 * GRID, 64 * ext_x), table(4 * GRID, 64 * ext_x), influence_s, turn_s, xsend)
            swap_dom(xsend, xrecv, xs_sem, xr_sem)

        @pl.when(i == edge_split[1])
        def _():
            dom_wait(xsend, xrecv, xs_sem, xr_sem, "wait_recv")
            inverse_y_step(xrecv, table(4 * GRID + 128 * ext_x, 4 * rows_back), turn_s, isend)
            for copy in i_copies:
                copy.start()
            irecv[part] = isend[part]

        pipe(2 * i, 2 * i + 1, buf=even_s, other=odd_s)
        pipe(2 * i + 1, 2 * i + 2, buf=odd_s, other=even_s)
        return carry

    lax.fori_loop(0, 15, edges, 0)
    pipe(30, 31, buf=even_s, other=odd_s)
    pipe(31, None, buf=odd_s, other=even_s)
    finish(new_ref, own_ref, inv_s, w_out)
    for copy in i_copies:
        copy.wait_recv()
    read_step(irecv, cell_s, frac_ref, along_s, table(2 * GRID, GRID), pot_ref, back_s)
    for copy in geo_copies + first + second + z_copies + i_copies:
        copy.wait_send()
    dom_wait(ysend, yrecv, ys_sem, yr_sem, "wait_send")
    dom_wait(xsend, xrecv, xs_sem, xr_sem, "wait_send")


def local(features, offsets, frac, neighbors, counts, w_src, w_dst, w_rad, w_mid, w_out, w_charge):
    f32, bf16 = jnp.float32, jnp.bfloat16
    flat = lax.optimization_barrier(neighbors.reshape(-1))
    operands = (
        flat, features[0, 0], flat.reshape(256, 128), counts.reshape(16, 128), offsets.reshape(48, 128),
        frac.reshape(48, 128), w_charge[None, :], w_src, w_dst, w_rad, w_mid, w_out, narrow, wide, wave_x, wave_yz,
    )
    vmem = pl.BlockSpec(memory_space=pltpu.VMEM)
    smem = pl.BlockSpec(memory_space=pltpu.SMEM)
    hbm = pl.BlockSpec(memory_space=pltpu.HBM)
    dma = pltpu.SemaphoreType.DMA
    slabs = pltpu.VMEM((4, 3 * rows_y + 40, 128), f32)
    pencils = pltpu.VMEM((64, 1, 1792), f32)
    backs = pltpu.VMEM((64, 16, 128), bf16)
    slabs_back = pltpu.VMEM((4, rows_back, 512), bf16)
    new_rows, potential = pl.pallas_call(
        layer_kernel,
        in_specs=[smem] + [hbm] * (len(operands) - 1),
        out_specs=(vmem, vmem),
        out_shape=(jax.ShapeDtypeStruct((2048, 128), bf16), jax.ShapeDtypeStruct((1, 2048), f32)),
        scratch_shapes=[
            pltpu.VMEM((9, head_rows, 128), bf16), pltpu.VMEM((8, 16, 128), f32),
            slabs, slabs, pencils, pencils, backs, backs, slabs_back, slabs_back,
            pltpu.VMEM((6144 + 2 * table_pad, 128), f32), pltpu.VMEM((2048, 128), f32), pltpu.VMEM((144, 128), f32),
            pltpu.VMEM((9, 256, 128), f32), pltpu.VMEM((256, 8, 128), f32), pltpu.VMEM((2048, 384), bf16),
            pltpu.VMEM((ext_x * rows_y, GRID), f32), pltpu.VMEM((8, 2048), f32), pltpu.VMEM((2, GRID, 2048), bf16),
            pltpu.VMEM((GRID, GRID), f32), pltpu.VMEM((48, 128), jnp.int32), pltpu.VMEM((16, 128), f32),
            pltpu.VMEM((1024, 128), f32), pltpu.VMEM((1024, 128), f32), pltpu.VMEM((64, 16, 128), f32),
            pltpu.VMEM((ext_x * rows_back, GRID), f32),
            *[pltpu.VMEM(x.shape, x.dtype) for x in operands[1:2] + operands[2:]], dma((15,)),
            dma((8,)), dma((9,)), dma((8,)), dma((8,)), dma((3,)), dma((3,)),
            dma((63,)), dma((63,)), dma((63,)), dma((63,)), dma((3,)), dma((3,)),
        ],
        compiler_params=pltpu.CompilerParams(
            vmem_limit_bytes=50 * 2**20, collective_id=0, has_side_effects=True
        ),
        name="layer",
    )(*operands)
    return new_rows.reshape(features.shape), potential.reshape(1, 1, 2048)


def solution(mesh):
    placed = (
        P("dom", "sub", None, None),
        P(None, "dom", "sub", None),
        P(None, "dom", "sub", None),
        P("dom", "sub", None, None),
        P("dom", "sub", None),
        P(),
        P(),
        P(),
        P(),
        P(),
        P(),
    )
    return jax.shard_map(
        local,
        mesh=mesh,
        in_specs=placed,
        out_specs=(P("dom", "sub", None, None), P("dom", "sub", None)),
        check_vma=False,
    )
```

time: 115 us -> 90.1 us (0.78)
  Pallas kernels: 98.9 us -> 86 us
  local copies, waits for them, and re-layouts: 11.7 us -> 3.12 us
  other arithmetic: 3.12 us -> 0 us
    pallas_call x1, Pallas kernels: 98.9 us -> 86 us  [local(): pl.pallas_call(layer_kernel, in_specs=[smem] + [hbm] * (len(operands) - 1...]
    another operation x2 -> x0, local copies, waits for them, and re-layouts: 1.96 us -> none  [the longest x1 1.66 us: local(): pairs.reshape(256, 128)]
    add x2 -> x0, local copies, waits for them, and re-layouts: 1.84 us -> none  [local(): square_y + square_z]
    unnamed x54 -> x29, local copies, waits for them, and re-layouts: 4.36 us -> 2.82 us
    dynamic_slice x1 -> x0, local copies, waits for them, and re-layouts: 1.41 us -> none  [local(): table.reshape(4, 64)[:, dom][:, None]]
where the time goes in v3:
time: 90.1 us; the launch traced here: 90 us
  Pallas kernels  86 us (95%)
  local copies, waits for them, and re-layouts  3.12 us (3%)
    pallas_call x1, Pallas kernels, local(): pl.pallas_call(layer_kernel, in_specs=[smem] + [hbm] * (len(operands) - 1...  86 us
    unnamed x29, local copies, waits for them, and re-layouts  2.82 us

profile of v3, /device:TPU:1, one launch (start us, length us, event | category | flops | bytes accessed | tf_op | source)
XLA Modules:
  0.0 90.0 jit_solution(3237991114202611606)
XLA Ops:
  0.6 0.0 copy-start.3
  0.6 0.0 copy-start.2
  0.7 0.0 copy-start
  0.7 0.0 copy-start.12
  0.7 0.0 copy-start.4
  0.7 0.0 copy-start.7
  0.7 0.0 copy-start.11
  0.7 0.0 copy-start.6
  0.7 0.0 copy-start.5
  0.7 0.0 copy-start.10
  0.7 0.0 copy-start.9
  0.8 0.0 copy-start.8
  0.8 0.0 copy-start.1
  0.8 1.4 %copy.17 = s32[1,1,2048,16]{3,2,1,0:T(8,128)S(1)} copy(s32[1,1,2048,16]{2,3,1,0:T(8,128)} %param.18) | data formatting | bytes 262144 | tf_op args[3]
  2.1 0.3 reshape.25.idx_ref
  2.5 0.0 copy-done.3
  2.5 0.0 copy-done.2
  2.5 0.0 copy-done
  2.5 0.0 copy-done.12
  2.5 0.0 copy-done.4
  2.5 0.0 copy-done.7
  2.5 0.0 copy-done.11
  2.5 0.0 copy-done.6
  2.5 0.0 copy-done.5
  2.5 0.0 copy-done.10
  2.6 0.0 copy-done.9
  2.6 0.0 copy-done.8
  2.6 0.0 copy-done.1
  2.6 86.0 %layer.1 = (bf16[2048,128]{1,0:T(8,128)(2,1)S(1)}, f32[1,2048]{1,0:T(1,128)S(1)}) custom-call(s32[32768]{0:T(1024)S(1)} %reshape.25.idx_ref, bf16[2048,128]{1,0:T(8,128)(2,1)S(1)} %bitcast.11, s32[256,128]{1,0:T(8,128)S(1)} %bitcast.10, s32[16,128]{1,0:T(8,128)S(1)} %bitcast.15, s32[48,128]{1,0:T(8,128)S(1)} %bitcast.13, f32[48,128]{1,0:T(8,128)S(1)} %bitcast.14, ...), custom_call_target="tpu_custom_call" | custom-call | tf_op jit(solution)/shard_map/layer/pallas_call | solution.py:569
  88.6 0.8 copy.20
  89.4 0.6 copy.21
Async XLA Ops:
  0.6 1.8 %copy-start.3 = (f32[144,256]{1,0:T(8,128)S(1)}, f32[144,256]{1,0:T(8,128)}, u32[]{:S(2)}) copy-start(f32[144,256]{1,0:T(8,128)} %constant.11.clone.wave_yz_hbm) | copy-start | bytes 442372
  0.6 1.8 %copy-start.2 = (f32[512,128]{1,0:T(8,128)S(1)}, f32[512,128]{1,0:T(8,128)}, u32[]{:S(2)}) copy-start(f32[512,128]{1,0:T(8,128)} %constant.10.clone.wave_x_hbm) | copy-start | bytes 786436
  0.7 1.8 %copy-start = (bf16[1024,512]{1,0:T(8,128)(2,1)S(1)}, bf16[1024,512]{1,0:T(8,128)(2,1)}, u32[]{:S(2)}) copy-start(bf16[1024,512]{1,0:T(8,128)(2,1)} %constant.9.clone.wide_hbm) | copy-start | bytes 3145732
  0.7 1.8 %copy-start.12 = (f32[128]{0:T(128)S(1)}, f32[128]{0:T(128)}, u32[]{:S(2)}) copy-start(f32[128]{0:T(128)} %param.25) | copy-start | bytes 1540
  0.7 1.8 %copy-start.4 = (bf16[384,128]{1,0:T(8,128)(2,1)S(1)}, bf16[384,128]{1,0:T(8,128)(2,1)}, u32[]{:S(2)}) copy-start(bf16[384,128]{1,0:T(8,128)(2,1)} %wout_hbm.1) | copy-start | bytes 294916
  0.7 1.8 %copy-start.7 = (bf16[128,128]{1,0:T(8,128)(2,1)S(1)}, bf16[128,128]{1,0:T(8,128)(2,1)}, u32[]{:S(2)}) copy-start(bf16[128,128]{1,0:T(8,128)(2,1)} %wmid_hbm.1) | copy-start | bytes 98308
  0.7 1.8 %copy-start.11 = (f32[8,128]{1,0:T(8,128)S(1)}, f32[8,128]{1,0:T(8,128)}, u32[]{:S(2)}) copy-start(f32[8,128]{1,0:T(8,128)} %wrad_hbm.1) | copy-start | bytes 12292
  0.7 1.8 %copy-start.6 = (bf16[128,128]{1,0:T(8,128)(2,1)S(1)}, bf16[128,128]{1,0:T(8,128)(2,1)}, u32[]{:S(2)}) copy-start(bf16[128,128]{1,0:T(8,128)(2,1)} %wdst_hbm.1) | copy-start | bytes 98308
  0.7 1.8 %copy-start.5 = (bf16[128,128]{1,0:T(8,128)(2,1)S(1)}, bf16[128,128]{1,0:T(8,128)(2,1)}, u32[]{:S(2)}) copy-start(bf16[128,128]{1,0:T(8,128)(2,1)} %wsrc_hbm.1) | copy-start | bytes 98308
  0.7 1.8 %copy-start.10 = (s32[1,1,2048]{2,1,0:T(1,128)S(1)}, s32[1,1,2048]{2,1,0:T(1,128)}, u32[]{:S(2)}) copy-start(s32[1,1,2048]{2,1,0:T(1,128)} %param.19) | copy-start | bytes 24580
  0.7 1.8 %copy-start.9 = (f32[3,1,1,2048]{3,2,1,0:T(1,128)S(1)}, f32[3,1,1,2048]{3,2,1,0:T(1,128)}, u32[]{:S(2)}) copy-start(f32[3,1,1,2048]{3,2,1,0:T(1,128)} %param.17) | copy-start | bytes 73732
  0.8 1.8 %copy-start.8 = (s32[3,1,1,2048]{3,2,1,0:T(1,128)S(1)}, s32[3,1,1,2048]{3,2,1,0:T(1,128)}, u32[]{:S(2)}) copy-start(s32[3,1,1,2048]{3,2,1,0:T(1,128)} %param.16) | copy-start | bytes 73732
  0.8 1.8 %copy-start.1 = (bf16[1,1,2048,128]{3,2,1,0:T(8,128)(2,1)S(1)}, bf16[1,1,2048,128]{3,2,1,0:T(8,128)(2,1)}, u32[]{:S(2)}) copy-start(bf16[1,1,2048,128]{3,2,1,0:T(8,128)(2,1)} %param.15) | copy-start | bytes 1572868

commit v4 on v3

--- a/solution.py
+++ b/solution.py
@@ -17,7 +17,7 @@
 rows_back = 80
 head_rows = 512
 table_pad = 8
-edge_split = (6, 11)
+edge_split = (7, 12)
 halo_places = [(0, 0), (0, 1), (0, 2), (1, 0), (1, 2), (2, 0), (2, 1), (2, 2)]
 
 
@@ -444,7 +444,7 @@
 
     def dom_copy(src, dst, send, recv, step):
         target = lax.rem(me + step, doms)
-        return remote(src.at[target], dst.at[me], send.at[step - 1], recv.at[step - 1], target, part)
+        return remote(src.at[target], dst.at[me], send.at[0], recv.at[0], target, part)
 
     def swap_dom(src, dst, send, recv):
         def start(step, carry):
@@ -455,11 +455,9 @@
         dst[me] = src[me]
 
     def dom_wait(src, dst, send, recv, which):
-        def wait(step, carry):
-            getattr(dom_copy(src, dst, send, recv, step), which)()
-            return carry
-
-        lax.fori_loop(1, doms, wait, 0)
+        every = pl.ds(0, doms - 1)
+        copy = remote(src.at[every], dst.at[every], send.at[0], recv.at[0], turn(me, 1, doms), part)
+        getattr(copy, which)()
 
     loads[4].wait()
     spread(cell_s, frac_ref, charge_s, along_s, grid_s, table(0, GRID), zsend)
@@ -503,7 +501,6 @@
         copy.wait_recv()
     forward_y_step(zrecv, broad(0, 4 * rows_y), ysend)
     swap_dom(ysend, yrecv, ys_sem, yr_sem)
-
     for slot in (0, 2, 3, 5, 6, 8):
         feat_wait(slot)
     for r, (place_x, place_y) in enumerate(halo_places):
@@ -582,7 +579,7 @@
             pltpu.VMEM((ext_x * rows_back, GRID), f32),
             *[pltpu.VMEM(x.shape, x.dtype) for x in operands[1:2] + operands[2:]], dma((15,)),
             dma((8,)), dma((9,)), dma((8,)), dma((8,)), dma((3,)), dma((3,)),
-            dma((63,)), dma((63,)), dma((63,)), dma((63,)), dma((3,)), dma((3,)),
+            dma((1,)), dma((1,)), dma((1,)), dma((1,)), dma((3,)), dma((3,)),
         ],
         compiler_params=pltpu.CompilerParams(
             vmem_limit_bytes=50 * 2**20, collective_id=0, has_side_effects=True

time: 90.1 us -> 86.2 us (0.957)
  Pallas kernels: 86 us -> 82.1 us
    pallas_call x1, Pallas kernels: 86 us -> 82.1 us  [local(): pl.pallas_call(layer_kernel, in_specs=[smem] + [hbm] * (len(operands) - 1...]
where the time goes in v4:
time: 86.2 us; the launch traced here: 86.1 us
  Pallas kernels  82.1 us (95%)
  local copies, waits for them, and re-layouts  3.12 us (4%)
    pallas_call x1, Pallas kernels, local(): pl.pallas_call(layer_kernel, in_specs=[smem] + [hbm] * (len(operands) - 1...  82.1 us
    unnamed x29, local copies, waits for them, and re-layouts  2.82 us

profile of v4, /device:TPU:1, one launch (start us, length us, event | category | flops | bytes accessed | tf_op | source)
XLA Modules:
  0.0 86.1 jit_solution(17789483165924156934)
XLA Ops:
  0.6 0.0 copy-start.3
  0.6 0.0 copy-start.2
  0.7 0.0 copy-start
  0.7 0.0 copy-start.12
  0.7 0.0 copy-start.4
  0.7 0.0 copy-start.7
  0.7 0.0 copy-start.11
  0.7 0.0 copy-start.6
  0.7 0.0 copy-start.5
  0.7 0.0 copy-start.10
  0.7 0.0 copy-start.9
  0.8 0.0 copy-start.8
  0.8 0.0 copy-start.1
  0.8 1.4 %copy.17 = s32[1,1,2048,16]{3,2,1,0:T(8,128)S(1)} copy(s32[1,1,2048,16]{2,3,1,0:T(8,128)} %param.18) | data formatting | bytes 262144 | tf_op args[3]
  2.1 0.3 reshape.25.idx_ref
  2.5 0.0 copy-done.3
  2.5 0.0 copy-done.2
  2.5 0.0 copy-done
  2.5 0.0 copy-done.12
  2.5 0.0 copy-done.4
  2.5 0.0 copy-done.7
  2.5 0.0 copy-done.11
  2.5 0.0 copy-done.6
  2.5 0.0 copy-done.5
  2.5 0.0 copy-done.10
  2.6 0.0 copy-done.9
  2.6 0.0 copy-done.8
  2.6 0.0 copy-done.1
  2.6 82.1 %layer.1 = (bf16[2048,128]{1,0:T(8,128)(2,1)S(1)}, f32[1,2048]{1,0:T(1,128)S(1)}) custom-call(s32[32768]{0:T(1024)S(1)} %reshape.25.idx_ref, bf16[2048,128]{1,0:T(8,128)(2,1)S(1)} %bitcast.11, s32[256,128]{1,0:T(8,128)S(1)} %bitcast.10, s32[16,128]{1,0:T(8,128)S(1)} %bitcast.15, s32[48,128]{1,0:T(8,128)S(1)} %bitcast.13, f32[48,128]{1,0:T(8,128)S(1)} %bitcast.14, ...), custom_call_target="tpu_custom_call" | custom-call | tf_op jit(solution)/shard_map/layer/pallas_call | solution.py:566
  84.7 0.8 copy.20
  85.5 0.6 copy.21
Async XLA Ops:
  0.6 1.8 %copy-start.3 = (f32[144,256]{1,0:T(8,128)S(1)}, f32[144,256]{1,0:T(8,128)}, u32[]{:S(2)}) copy-start(f32[144,256]{1,0:T(8,128)} %constant.11.clone.wave_yz_hbm) | copy-start | bytes 442372
  0.6 1.8 %copy-start.2 = (f32[512,128]{1,0:T(8,128)S(1)}, f32[512,128]{1,0:T(8,128)}, u32[]{:S(2)}) copy-start(f32[512,128]{1,0:T(8,128)} %constant.10.clone.wave_x_hbm) | copy-start | bytes 786436
  0.7 1.8 %copy-start = (bf16[1024,512]{1,0:T(8,128)(2,1)S(1)}, bf16[1024,512]{1,0:T(8,128)(2,1)}, u32[]{:S(2)}) copy-start(bf16[1024,512]{1,0:T(8,128)(2,1)} %constant.9.clone.wide_hbm) | copy-start | bytes 3145732
  0.7 1.8 %copy-start.12 = (f32[128]{0:T(128)S(1)}, f32[128]{0:T(128)}, u32[]{:S(2)}) copy-start(f32[128]{0:T(128)} %param.25) | copy-start | bytes 1540
  0.7 1.8 %copy-start.4 = (bf16[384,128]{1,0:T(8,128)(2,1)S(1)}, bf16[384,128]{1,0:T(8,128)(2,1)}, u32[]{:S(2)}) copy-start(bf16[384,128]{1,0:T(8,128)(2,1)} %wout_hbm.1) | copy-start | bytes 294916
  0.7 1.8 %copy-start.7 = (bf16[128,128]{1,0:T(8,128)(2,1)S(1)}, bf16[128,128]{1,0:T(8,128)(2,1)}, u32[]{:S(2)}) copy-start(bf16[128,128]{1,0:T(8,128)(2,1)} %wmid_hbm.1) | copy-start | bytes 98308
  0.7 1.8 %copy-start.11 = (f32[8,128]{1,0:T(8,128)S(1)}, f32[8,128]{1,0:T(8,128)}, u32[]{:S(2)}) copy-start(f32[8,128]{1,0:T(8,128)} %wrad_hbm.1) | copy-start | bytes 12292
  0.7 1.8 %copy-start.6 = (bf16[128,128]{1,0:T(8,128)(2,1)S(1)}, bf16[128,128]{1,0:T(8,128)(2,1)}, u32[]{:S(2)}) copy-start(bf16[128,128]{1,0:T(8,128)(2,1)} %wdst_hbm.1) | copy-start | bytes 98308
  0.7 1.8 %copy-start.5 = (bf16[128,128]{1,0:T(8,128)(2,1)S(1)}, bf16[128,128]{1,0:T(8,128)(2,1)}, u32[]{:S(2)}) copy-start(bf16[128,128]{1,0:T(8,128)(2,1)} %wsrc_hbm.1) | copy-start | bytes 98308
  0.7 1.8 %copy-start.10 = (s32[1,1,2048]{2,1,0:T(1,128)S(1)}, s32[1,1,2048]{2,1,0:T(1,128)}, u32[]{:S(2)}) copy-start(s32[1,1,2048]{2,1,0:T(1,128)} %param.19) | copy-start | bytes 24580
  0.7 1.8 %copy-start.9 = (f32[3,1,1,2048]{3,2,1,0:T(1,128)S(1)}, f32[3,1,1,2048]{3,2,1,0:T(1,128)}, u32[]{:S(2)}) copy-start(f32[3,1,1,2048]{3,2,1,0:T(1,128)} %param.17) | copy-start | bytes 73732
  0.8 1.8 %copy-start.8 = (s32[3,1,1,2048]{3,2,1,0:T(1,128)S(1)}, s32[3,1,1,2048]{3,2,1,0:T(1,128)}, u32[]{:S(2)}) copy-start(s32[3,1,1,2048]{3,2,1,0:T(1,128)} %param.16) | copy-start | bytes 73732
  0.8 1.8 %copy-start.1 = (bf16[1,1,2048,128]{3,2,1,0:T(8,128)(2,1)S(1)}, bf16[1,1,2048,128]{3,2,1,0:T(8,128)(2,1)}, u32[]{:S(2)}) copy-start(bf16[1,1,2048,128]{3,2,1,0:T(8,128)(2,1)} %param.15) | copy-start | bytes 1572868
